TPU v7x, 512 devices: a whole 4x4x16 slice. The times are simulated.
512 devices in a mesh: cuts: 4 (over z_hi), dev: 128 (over z_lo, x, y, core).
Axes of the slice: x: 4, y: 4, z: 16 (z_hi: 4, z_lo: 4; z = z_hi * 4 + z_lo), core: 2. Of those that a mesh axis runs over, the one named last changes fastest.
Arguments:
- hidden: bfloat16 [65536, 13824], P(('cuts', 'dev')), may hold values from -6 to 6
- stream: bfloat16 [65536, 5120], P(('cuts', 'dev')), may hold values from -6 to 6
- adapter_in: bfloat16 [32, 13824], P(None, 'dev'), may hold values from -0.0546875 to 0.0546875
- adapter_out: bfloat16 [32, 5120], P(None, 'dev'), may hold values from -1 to 1
- norm_gain: float32 [1, 5120], P(None, 'dev'), may hold values from 0.5 to 1.5
- teacher: float32 [512], P(('cuts', 'dev')), may hold values from -4 to 4
Outputs:
- grad_in: float32 [32, 13824], P(None, 'dev')
- grad_out: float32 [32, 5120], P(None, 'dev')
- grad_gain: float32 [1, 5120], P(None, 'dev')
All inputs are finite; a program needn't handle non-finite values.
Results may differ from a plain program's by a relative error of at most 0.024.
Values may be sent and summed in bfloat16 or wider, within the bound.
No kernel may reach another device: no remote copies, remote signals or barrier semaphores. Data moves between devices by JAX's collectives and lax.ppermute only.
A program may use at most 64 MiB of HBM per device.

v0:
```python
import jax
import jax.numpy as jnp
from jax import lax
from jax.sharding import PartitionSpec as P

QLEN = 32
PLEN = 48


def local_grads(hidden, stream, adapter_in, adapter_out, norm_gain, teacher):
    groups = teacher.shape[0]
    seq_tok = QLEN + 2 * PLEN
    width = stream.shape[1]
    low_rank = jnp.dot(hidden, adapter_in.T, preferred_element_type=jnp.float32).astype(
        jnp.bfloat16
    )
    summed = stream.astype(jnp.float32) + jnp.dot(
        low_rank, adapter_out, preferred_element_type=jnp.float32
    )
    inv_rms = lax.rsqrt(jnp.mean(summed * summed, axis=-1, keepdims=True) + 1e-06)
    unit = summed * inv_rms
    normed = unit * norm_gain
    blocks = normed.reshape(groups, seq_tok, width)
    query = jnp.mean(blocks[:, :QLEN], axis=1)
    positive = jnp.mean(blocks[:, QLEN : QLEN + PLEN], axis=1)
    negative = jnp.mean(blocks[:, QLEN + PLEN :], axis=1)
    margin = jnp.sum(query * (positive - negative), axis=-1)
    error = (margin - teacher)[:, None]
    d_query = error * (positive - negative) / QLEN
    d_pos = error * query / PLEN
    d_neg = -error * query / PLEN
    d_normed = jnp.concatenate(
        [
            jnp.broadcast_to(d_query[:, None], (groups, QLEN, width)),
            jnp.broadcast_to(d_pos[:, None], (groups, PLEN, width)),
            jnp.broadcast_to(d_neg[:, None], (groups, PLEN, width)),
        ],
        axis=1,
    ).reshape(groups * seq_tok, width)
    grad_gain = jnp.sum(d_normed * unit, axis=0, keepdims=True)
    d_unit = d_normed * norm_gain
    d_summed = ((d_unit - unit * jnp.mean(d_unit * unit, axis=-1, keepdims=True)) * inv_rms).astype(
        jnp.bfloat16
    )
    grad_out = jnp.dot(low_rank.T, d_summed, preferred_element_type=jnp.float32)
    d_low = jnp.dot(d_summed, adapter_out.T, preferred_element_type=jnp.float32).astype(
        jnp.bfloat16
    )
    grad_in = jnp.dot(d_low.T, hidden, preferred_element_type=jnp.float32)
    return (grad_in, grad_out, grad_gain)


def body(hidden, stream, adapter_in, adapter_out, norm_gain, teacher):
    whole_in, whole_out, whole_gain = (
        lax.all_gather(adapter_in, "dev", axis=1, tiled=True),
        lax.all_gather(adapter_out, "dev", axis=1, tiled=True),
        lax.all_gather(norm_gain.astype(jnp.bfloat16), "dev", axis=1, tiled=True).astype(
            norm_gain.dtype
        ),
    )
    terms = local_grads(hidden, stream, whole_in, whole_out, whole_gain, teacher)
    shares = (
        lax.psum_scatter(terms[0], "dev", scatter_dimension=1, tiled=True),
        lax.psum_scatter(terms[1], "dev", scatter_dimension=1, tiled=True),
        lax.psum_scatter(terms[2], "dev", scatter_dimension=1, tiled=True),
    )
    result = lax.psum((shares[0], shares[1], shares[2]), "cuts")
    return (result[0], result[1], result[2])


def solution(mesh):
    return jax.shard_map(
        body,
        mesh=mesh,
        in_specs=(
            P(("cuts", "dev"), None),
            P(("cuts", "dev"), None),
            P(None, "dev"),
            P(None, "dev"),
            P(None, "dev"),
            P(("cuts", "dev")),
        ),
        out_specs=(P(None, "dev"), P(None, "dev"), P(None, "dev")),
        check_vma=False,
    )
```

profile of v0, /device:TPU:128, one launch (start us, length us, event | category | flops | bytes accessed | tf_op | source)
XLA Modules:
  0.0 2391.5 jit_solution(11541367405893442992)
XLA Ops:
  7.2 0.0 copy-start
  7.2 0.0 all-reduce.8.cloned.1.call-start
  7.2 0.8 convert_bitcast_fusion
  8.0 1.5 fusion.9
  10.2 0.2 dynamic-update-slice
  10.4 672.3 %all-reduce = bf16[5120]{0:T(1024)(128)(2,1)} all-reduce(bf16[5120]{0:T(1024)(128)(2,1)S(1)} %dynamic-update-slice), channel_id=1, replica_groups=mesh['cuts'=4,'dev'=128] {'dev'}, use_global_device_ids=true, to_apply=%add | all-reduce | flops 5120 | bytes 20480
  682.8 0.0 copy-start.9
  682.8 1.3 mul.133
  684.1 182.6 %all-gather = bf16[128,108,32]{1,2,0:T(8,128)(2,1)S(1)} all-gather(bf16[1,108,32]{1,2,0:T(8,128)(2,1)} %bitcast.54), channel_id=1, replica_groups=mesh['cuts'=4,'dev'=128] {'dev'}, dimensions={0}, use_global_device_ids=true | all-gather | bytes 891648 | tf_op jit(solution)/shard_map/all_gather | solution.py:55
  866.7 1.4 copy.11
  868.1 3.6 reshape.97
  871.7 0.0 copy-done.9
  871.7 184.3 %all-gather.1 = bf16[128,40,32]{1,2,0:T(8,128)(2,1)S(1)} all-gather(bf16[1,40,32]{1,2,0:T(8,128)(2,1)S(1)} %bitcast.55), channel_id=1, replica_groups=mesh['cuts'=4,'dev'=128] {'dev'}, dimensions={0}, use_global_device_ids=true | all-gather | bytes 330240 | tf_op jit(solution)/shard_map/all_gather | solution.py:56
  1056.0 1.4 copy.12
  1057.4 3.5 reshape.99
  1060.9 0.0 copy-done
  1060.9 0.0 copy-start.4
  1060.9 0.0 copy-start.5
  1060.9 2.5 convolution_convert_fusion.1
  1063.4 0.0 copy-done.4
  1063.4 0.0 copy-done.5
  1063.4 0.0 copy-start.6
  1063.4 0.6 multiply_reduce_fusion
  1064.0 0.0 copy-start.1
  1064.1 0.1 copy-done.6
  1064.1 0.3 multiply_bitcast_fusion
  1064.5 1.1 copy-done.1
  1065.6 0.1 slice_reduce_fusion.2
  1065.6 0.0 copy-start.8
  1065.6 0.2 slice_reduce_fusion.1
  1066.4 0.0 copy-done.8
  1066.5 0.6 multiply_reduce_fusion.1
  1067.7 0.6 multiply_multiply_fusion.2
  1068.3 0.0 copy-start.2
  1068.3 0.0 copy-start.7
  1068.3 0.9 multiply_multiply_fusion.1
  1069.2 0.8 broadcast_in_dim.8
  1070.0 0.1 broadcast_in_dim.9
  1070.1 0.1 broadcast_in_dim.10
  1070.1 0.0 copy-done.2
  1070.1 0.0 copy-done.7
  1070.1 1.5 fusion.7
  1071.6 0.6 fusion.6
  1072.3 0.0 copy-start.3
  1072.3 1.1 copy-done.3
  1073.3 1.2 fusion.10
  1074.5 4.3 fusion.8
  1078.8 0.0 all-reduce.8.cloned.1.call-update
  1080.1 663.9 %all-reduce.3 = f32[1,5120]{1,0:T(1,128)} all-reduce(f32[1,5120]{1,0:T(1,128)} %bitcast.53), channel_id=4, replica_groups=mesh['cuts'=4,'dev'=128] {'dev'}, use_global_device_ids=true, to_apply=%region_11.0.clone | all-reduce | flops 5120 | bytes 40960
  1744.0 1.2 constant_dynamic-slice_fusion
  1745.3 613.0 %all-reduce.8.cloned.1.call-done = (f32[32,13824]{1,0:T(8,128)}, f32[32,5120]{1,0:T(8,128)}) async-done(((f32[32,13824]{1,0:T(8,128)}, f32[32,5120]{1,0:T(8,128)}), (f32[32,13824]{1,0:T(8,128)}, f32[32,5120]{1,0:T(8,128)})) %all-reduce.8.cloned.1.call-update) | async-done | bytes 2424848
  2358.2 0.8 constant_dynamic-slice_fusion.1
  2359.1 1.4 constant_dynamic-slice_fusion.2
  2360.5 24.1 %all-reduce.5 = (f32[32,108]{1,0:T(8,128)}, f32[32,40]{1,0:T(8,128)}, f32[1,40]{1,0:T(1,128)}) all-reduce(f32[32,108]{1,0:T(8,128)} %constant_dynamic-slice_fusion.2, f32[32,40]{1,0:T(8,128)S(1)} %constant_dynamic-slice_fusion.1, f32[1,40]{1,0:T(1,128)} %constant_dynamic-slice_fusion), channel_id=1, replica_groups=mesh['cuts'=4,'dev'=128] {'cuts'}, use_global_device_ids=true, to_apply=%region_7.0 | all-reduce | flops 4776 | bytes 38208 | tf_op jit(solution)/shard_map/psum | solution.py:67
  (3 shorter events, 0.0 us)
Async XLA Ops:
  7.2 1053.7 %copy-start = (bf16[128,13824]{1,0:T(8,128)(2,1)S(1)}, bf16[128,13824]{1,0:T(8,128)(2,1)}, u32[]{:S(2)}) copy-start(bf16[128,13824]{1,0:T(8,128)(2,1)} %param.6) | copy-start | bytes 10616836
  7.2 2351.1 %all-reduce.8.cloned.1.call-start = ((), (), s32[]{:S(2)}) async-start(), calls=%async_computation | async-start | bytes 4849664
  682.8 188.9 %copy-start.9 = (bf16[32,40]{1,0:T(8,128)(2,1)S(1)}, bf16[32,40]{1,0:T(8,128)(2,1)}, u32[]{:S(2)}) copy-start(bf16[32,40]{1,0:T(8,128)(2,1)} %param.9) | copy-start | bytes 7684
  1060.9 2.5 copy-start.4
  1060.9 2.5 copy-start.5
  1063.4 0.7 copy-start.6
  1064.0 1.5 copy-start.1
  1065.6 0.8 copy-start.8
  1068.3 1.8 copy-start.2
  1068.3 1.8 copy-start.7
  1072.3 1.1 copy-start.3
Sparse Core Ops, SparseCore 0:
  1078.9 1279.2 all-reduce.7
where the time goes:
time: 2390 us
  blocking collectives  1730 us (72%)
  waiting for transfers between devices  613 us (26%)
    unnamed x2, blocking collectives  1340 us
    unnamed x2, waiting for transfers between devices  613 us
    all_gather x1, blocking collectives, body(): lax.all_gather(adapter_out, 'dev', axis=1, tiled=True)  184 us
    all_gather x1, blocking collectives, body(): lax.all_gather(adapter_in, 'dev', axis=1, tiled=True)  183 us
  transfers between devices with their start and end apart: 1, of which 1 were waited for; matrix products, arithmetic and copies ran while one was open for 0% of the time, Pallas kernels for 0%

commit v1 on v0

v1 whole, which is shorter than its diff:
```python
import jax
import jax.numpy as jnp
from jax import lax
from jax.experimental import pallas as pl
from jax.experimental.pallas import tpu as pltpu
from jax.sharding import Mesh, PartitionSpec as P

QLEN = 32
PLEN = 48
TOK = QLEN + 2 * PLEN
D = 5120
FF = 13824
R = 32
NZ, NX, NY, NC = 4, 4, 4, 2
NXY = NX * NY
WF = FF // (NZ * NXY * NC)
WD = D // (NZ * NXY * NC)
HD = WD // 2
FZ = FF // NZ
DZ = D // NZ
BLK = 40
LANE = 128
STEP = 512
DEV = ("zl", "x", "y", "c")
ALL = ("zh",) + DEV
f32 = jnp.float32
bf16 = jnp.bfloat16


def lanes(rows):
    return lax.broadcasted_iota(jnp.int32, (rows, LANE), 1)


def roll(value, shift):
    shift %= LANE
    return value if shift == 0 else pltpu.roll(value, shift, axis=1)


def block_of(a, left, tail):
    top = jnp.where(lanes(R) < WF, a, left)
    n = lanes(8)
    low = tail[3]
    for g in (2, 1, 0):
        low = jnp.where(n < HD * (g + 1), tail[g], low)
    low = jnp.where(n >= 4 * HD, tail[4], low)
    return jnp.concatenate([top, low], axis=0)


def pack_kernel(a_ref, o_ref, g_ref, out_ref, a_s, o_s, g_s):
    a_s[...] = jnp.zeros_like(a_s)
    o_s[...] = jnp.zeros_like(o_s)
    g_s[...] = jnp.zeros_like(g_s)
    a_s[:, :WF] = a_ref[...].astype(f32)
    o_s[:, :WD] = o_ref[...].astype(f32)
    g_s[:, :WD] = jnp.broadcast_to(g_ref[...], (8, WD))
    o = o_s[...]
    tail = [roll(o[8 * g : 8 * g + 8], HD * g - HD) for g in range(4)]
    tail.append(roll(g_s[...], 4 * HD))
    b = block_of(a_s[...], roll(o, WF), tail)
    two = jnp.concatenate([b, b], axis=0).astype(bf16)
    for k in range(NZ * NC // 2):
        out_ref[2 * BLK * k : 2 * BLK * (k + 1), :] = two


def window(ref, rows, base, lo, width, at):
    t, s = divmod(lo, LANE)
    tile = ref[rows, pl.ds(pl.multiple_of(base + LANE * t, LANE), LANE)]
    if s + width > LANE:
        nxt = ref[rows, pl.ds(pl.multiple_of(base + LANE * (t + 1), LANE), LANE)]
        tile = jnp.where(lanes(tile.shape[0]) >= s, tile, nxt)
    return roll(tile, at - s)


class Tiles:
    def __init__(self, rows, emit):
        self.rows, self.emit, self.tile, self.t = rows, emit, None, 0

    def add(self, piece, at, lo, width):
        t, s = divmod(lo, LANE)
        moved = roll(piece, s - at)
        if t == self.t and self.tile is not None:
            self.tile = jnp.where(lanes(self.rows) >= s, moved, self.tile)
        else:
            self.t, self.tile = t, moved
        if s + width >= LANE:
            self.emit(t, self.tile)
            self.t, self.tile = t + 1, (moved if s + width > LANE else None)


def main_kernel(
    teacher_ref, msg_ref, hidden_hbm, stream_hbm, send_ref, keep_ref,
    hidden, stream, a_in, a_out, gain, unit, rows, grad_in, grad_out, grad_gain, sems,
):
    get_hidden = pltpu.make_async_copy(hidden_hbm, hidden, sems.at[0])
    get_stream = pltpu.make_async_copy(stream_hbm, stream, sems.at[1])
    get_hidden.start()
    get_stream.start()
    core = lax.axis_index("c")

    @pl.loop(0, NZ)
    def _(z):
        def put_in(t, tile):
            a_in[:, pl.ds(pl.multiple_of(z * FZ + LANE * t, LANE), LANE)] = tile.astype(bf16)

        def put_out(t, tile):
            a_out[:, pl.ds(pl.multiple_of(z * DZ + LANE * t, LANE), LANE)] = tile.astype(bf16)

        def put_gain(t, tile):
            gain[:, pl.ds(pl.multiple_of(z * DZ + LANE * t, LANE), LANE)] = tile

        ins, outs, gains = Tiles(R, put_in), Tiles(R, put_out), Tiles(8, put_gain)
        for i in range(NXY):
            at = pl.multiple_of((i * NZ + z) * (NC * BLK), NC * BLK)
            pair = msg_ref[pl.ds(at, NC * BLK), :].astype(f32)
            for c in range(NC):
                b = pair[BLK * c : BLK * c + BLK]
                ins.add(b[:R], 0, WF * (NC * i + c), WF)
                lo = WD * (NC * i + c)
                outs.add(b[:R], WF, lo, HD)
                low = b[R:]
                outs.add(
                    jnp.concatenate([roll(low, -HD * g) for g in range(4)], axis=0),
                    0, lo + HD, HD,
                )
                gains.add(low, 4 * HD, lo, WD)

    get_hidden.wait()

    def low_step(z, acc):
        cols = pl.ds(pl.multiple_of(z * FZ, LANE), FZ)
        return acc + lax.dot_general(
            hidden[:, cols], a_in[:, cols], (((1,), (1,)), ((), ())), preferred_element_type=f32
        )

    low = lax.fori_loop(0, NZ, low_step, jnp.zeros((TOK, R), f32)).astype(bf16)
    get_stream.wait()

    def sum_step(k, acc):
        cols = pl.ds(pl.multiple_of(k * STEP, LANE), STEP)
        s = stream[:, cols].astype(f32) + jnp.dot(low, a_out[:, cols], preferred_element_type=f32)
        unit[:, cols] = s
        for t in range(STEP // LANE):
            x = s[:, LANE * t : LANE * (t + 1)]
            acc = acc + x * x
        return acc

    squares = lax.fori_loop(0, D // STEP, sum_step, jnp.zeros((TOK, LANE), f32))
    inv = lax.rsqrt(jnp.sum(squares, axis=1, keepdims=True) / D + 1e-06)

    def unit_step(k, carry):
        margin, acc = carry
        cols = pl.ds(pl.multiple_of(k * STEP, LANE), STEP)
        u = unit[:, cols] * inv
        unit[:, cols] = u
        g = gain[:1, cols]
        uq = jnp.sum(u[:QLEN], axis=0, keepdims=True) / QLEN
        up = jnp.sum(u[QLEN : QLEN + PLEN], axis=0, keepdims=True) / PLEN
        un = jnp.sum(u[QLEN + PLEN :], axis=0, keepdims=True) / PLEN
        q = g * uq
        pn = g * (up - un)
        margin = margin + q * pn
        wq = pn * g / QLEN
        wp = q * g / PLEN
        rows[0:1, cols] = wq
        rows[1:2, cols] = wp
        rows[2:3, cols] = uq * pn
        prod = jnp.concatenate(
            [u[:QLEN] * wq, u[QLEN : QLEN + PLEN] * wp, u[QLEN + PLEN :] * -wp], axis=0
        )
        for t in range(STEP // LANE):
            acc = acc + prod[:, LANE * t : LANE * (t + 1)]
        return margin, acc

    margin, acc = lax.fori_loop(
        0, D // STEP, unit_step, (jnp.zeros((1, STEP), f32), jnp.zeros((TOK, LANE), f32))
    )
    err = jnp.sum(margin, axis=1, keepdims=True) - teacher_ref[0]
    mean = jnp.sum(acc, axis=1, keepdims=True) / D
    scale = inv * err

    def grad_step(k, acc):
        cols = pl.ds(pl.multiple_of(k * STEP, LANE), STEP)
        um = unit[:, cols] * mean
        wq = rows[0:1, cols]
        wp = rows[1:2, cols]
        d = jnp.concatenate(
            [wq - um[:QLEN], wp - um[QLEN : QLEN + PLEN], -wp - um[QLEN + PLEN :]], axis=0
        )
        d = (d * scale).astype(bf16)
        grad_out[:, cols] = lax.dot_general(
            low, d, (((0,), (0,)), ((), ())), preferred_element_type=f32
        )
        grad_gain[:, cols] = jnp.broadcast_to(2.0 * err * rows[2:3, cols], (8, STEP))
        return acc + lax.dot_general(
            d, a_out[:, cols], (((1,), (1,)), ((), ())), preferred_element_type=f32
        )

    d_low = lax.fori_loop(0, D // STEP, grad_step, jnp.zeros((TOK, R), f32)).astype(bf16)

    @pl.loop(0, NZ)
    def _(z):
        cols = pl.ds(pl.multiple_of(z * FZ, LANE), FZ)
        grad_in[:, cols] = lax.dot_general(
            d_low, hidden[:, cols], (((0,), (0,)), ((), ())), preferred_element_type=f32
        )

    @pl.loop(0, NZ // 2)
    def _(h):
        every = slice(None)
        for i in range(NXY):
            blocks = []
            for c in range(NC):
                pair = []
                for z2 in range(2):
                    z = 2 * h + z2
                    lo = WD * (NC * i + c)
                    a = window(grad_in, every, z * FZ, WF * (NC * i + c), WF, 0)
                    left = window(grad_out, every, z * DZ, lo, HD, WF)
                    tail = [
                        window(grad_out, slice(8 * g, 8 * g + 8), z * DZ, lo + HD, HD, HD * g)
                        for g in range(4)
                    ]
                    tail.append(window(grad_gain, every, z * DZ, lo, WD, 4 * HD))
                    pair.append(block_of(a, left, tail))
                blocks.append(jnp.concatenate(pair, axis=0))
            at = pl.ds(pl.multiple_of(NZ * BLK * i + 2 * BLK * h, 2 * BLK), 2 * BLK)
            first = core == 0
            send_ref[at, :] = jnp.where(first, blocks[1], blocks[0]).astype(bf16)
            keep_ref[at, :] = jnp.where(first, blocks[0], blocks[1]).astype(bf16)


def sum_xy_kernel(in_ref, out_ref):
    n = NZ * BLK
    acc = in_ref[:n].astype(f32)
    for k in range(1, NXY):
        acc = acc + in_ref[n * k : n * (k + 1)].astype(f32)
    out_ref[...] = acc.astype(bf16)


def sum_four(in_ref):
    x = in_ref[...].astype(f32)
    return (x[:BLK] + x[BLK : 2 * BLK]) + (x[2 * BLK : 3 * BLK] + x[3 * BLK :])


def sum_z_kernel(in_ref, out_ref):
    acc = sum_four(in_ref)
    out_ref[...] = jnp.concatenate([acc] * 4, axis=0).astype(bf16)


def final_kernel(in_ref, a_ref, o_ref, g_ref):
    b = sum_four(in_ref)
    low = b[R:]
    a_ref[...] = b[:R, :WF]
    left = roll(b[:R], -WF)
    right = jnp.concatenate([roll(low, HD - HD * g) for g in range(4)], axis=0)
    o_ref[...] = jnp.where(lanes(R) < HD, left, right)[:, :WD]
    g_ref[...] = roll(low, -4 * HD)[:1, :WD]


VMEM = pl.BlockSpec(memory_space=pltpu.VMEM)
ANY = pl.BlockSpec(memory_space=pl.ANY)
SMEM = pl.BlockSpec(memory_space=pltpu.SMEM)


def call(kernel, shapes, *args, specs=None, scratch=(), limit=None):
    return pl.pallas_call(
        kernel,
        out_shape=shapes,
        in_specs=specs or [VMEM] * len(args),
        out_specs=jax.tree.map(lambda _: VMEM, shapes),
        scratch_shapes=list(scratch),
        compiler_params=pltpu.CompilerParams(vmem_limit_bytes=limit) if limit else None,
    )(*args)


def shape(rows, cols, dtype=bf16):
    return jax.ShapeDtypeStruct((rows, cols), dtype)


def body(hidden, stream, adapter_in, adapter_out, norm_gain, teacher):
    mine = call(
        pack_kernel, shape(NZ * NC * BLK, LANE), adapter_in, adapter_out, norm_gain,
        scratch=[pltpu.VMEM((R, LANE), f32), pltpu.VMEM((R, LANE), f32), pltpu.VMEM((8, LANE), f32)],
    )
    column = lax.all_to_all(mine, ("zl", "c"), 0, 0, tiled=True)
    copies = jnp.broadcast_to(column[None], (NXY, NZ * NC * BLK, LANE))
    msg = lax.all_to_all(copies, ("x", "y"), 0, 0, tiled=True)
    msg = msg.reshape(NXY * NZ * NC * BLK, LANE)
    half = NXY * NZ * BLK
    send, keep = call(
        main_kernel, (shape(half, LANE), shape(half, LANE)), teacher, msg, hidden, stream,
        specs=[SMEM, VMEM, ANY, ANY],
        scratch=[
            pltpu.VMEM((TOK, FF), bf16),
            pltpu.VMEM((TOK, D), bf16),
            pltpu.VMEM((R, FF), bf16),
            pltpu.VMEM((R, D), bf16),
            pltpu.VMEM((8, D), f32),
            pltpu.VMEM((TOK, D), f32),
            pltpu.VMEM((8, D), f32),
            pltpu.VMEM((R, FF), f32),
            pltpu.VMEM((R, D), f32),
            pltpu.VMEM((8, D), f32),
            pltpu.SemaphoreType.DMA((2,)),
        ],
        limit=40 * 2**20,
    )
    other = lax.ppermute(send, "c", [(0, 1), (1, 0)])
    pairs = (keep.astype(f32) + other.astype(f32)).astype(bf16)
    parts = lax.all_to_all(pairs, ("x", "y"), 0, 0, tiled=True)
    part = call(sum_xy_kernel, shape(NZ * BLK, LANE), parts)
    part = lax.all_to_all(part, "zl", 0, 0, tiled=True)
    part = call(sum_z_kernel, shape(4 * BLK, LANE), part)
    part = lax.all_to_all(part, "zh", 0, 0, tiled=True)
    return call(final_kernel, (shape(R, WF, f32), shape(R, WD, f32), shape(1, WD, f32)), part)


def solution(mesh):
    fine = Mesh(mesh.devices.reshape(4, NZ, NX, NY, NC), ALL)
    return jax.shard_map(
        body,
        mesh=fine,
        in_specs=(P(ALL, None), P(ALL, None), P(None, DEV), P(None, DEV), P(None, DEV), P(ALL)),
        out_specs=(P(None, DEV), P(None, DEV), P(None, DEV)),
        check_vma=False,
    )
```

time: 2390 us -> 120 us (0.05)
  the two profiles are of different devices: /device:TPU:128 before, /device:TPU:32 now
where the time goes in v1:
time: 120 us
  blocking collectives  65.5 us (55%)
  waiting for transfers between devices  22.1 us (18%)
  Pallas kernels  20.8 us (17%)
  starting transfers between devices  6.35 us (5%)
  local copies, waits for them, and re-layouts  3.33 us (3%)
  between operations  1.31 us (1%)
    all_to_all x1, blocking collectives, body(): part = lax.all_to_all(part, 'zh', 0, 0, tiled=True)  25.8 us
    pallas_call x5, Pallas kernels, call(): pl.pallas_call(kernel, out_shape=shapes, in_specs=specs or [VMEM] * len(a...  20.8 us
    all_to_all x1, waiting for transfers between devices, body(): msg = lax.all_to_all(copies, ('x', 'y'), 0, 0, tiled=True)  20 us
    all_to_all x1, blocking collectives, body(): parts = lax.all_to_all(pairs, ('x', 'y'), 0, 0, tiled=True)  16.6 us
    all_to_all x1, blocking collectives, body(): column = lax.all_to_all(mine, ('zl', 'c'), 0, 0, tiled=True)  13.6 us
    all_to_all x1, blocking collectives, body(): part = lax.all_to_all(part, 'zl', 0, 0, tiled=True)  9.53 us
    all_to_all x1, starting transfers between devices, body(): msg = lax.all_to_all(copies, ('x', 'y'), 0, 0, tiled=True)  4.43 us
  transfers between devices with their start and end apart: 2, of which 2 were waited for; matrix products, arithmetic and copies ran while one was open for 0% of the time, Pallas kernels for 0%

profile of v1, /device:TPU:32, one launch (start us, length us, event | category | flops | bytes accessed | tf_op | source)
XLA Modules:
  0.0 119.6 jit_solution(3377608981575116835)
XLA Ops:
  0.6 1.4 %shard_map.85 = bf16[320,128]{1,0:T(8,128)(2,1)} custom-call(bf16[32,108]{1,0:T(8,128)(2,1)} %a_ref.1, bf16[32,40]{1,0:T(8,128)(2,1)} %o_ref.1, f32[1,40]{1,0:T(1,128)} %g_ref.1), custom_call_target="tpu_custom_call" | custom-call | tf_op jit(solution)/shard_map/pallas_call | solution.py:266
  2.1 13.6 %all_to_all.47 = bf16[8,40,128]{2,1,0:T(8,128)(2,1)S(1)} all-to-all(bf16[8,40,128]{2,1,0:T(8,128)(2,1)} %bitcast.12), channel_id=1, replica_groups=mesh['zh'=4,'zl'=4,'x'=4,'y'=4,'c'=2] {'zl','c'}, dimensions={0} | all-to-all | bytes 163840 | tf_op jit(solution)/shard_map/all_to_all | solution.py:285
  15.7 1.3 %broadcast_in_dim.9 = bf16[16,320,128]{2,1,0:T(8,128)(2,1)} broadcast(bf16[320,128]{1,0:T(8,128)(2,1)S(1)} %bitcast.13), dimensions={1,2} | broadcast | bytes 1392640 | tf_op jit(solution)/shard_map/broadcast_in_dim | solution.py:286
  17.0 0.0 copy-start.1
  17.0 4.4 %all-to-all-start.1 = ((bf16[16,320,128]{2,1,0:T(8,128)(2,1)}), bf16[16,320,128]{2,1,0:T(8,128)(2,1)S(1)}, u32[]{:S(2)}, u32[]{:S(2)}) async-start(bf16[16,320,128]{2,1,0:T(8,128)(2,1)} %broadcast_in_dim.9), calls=%async_computation.1 | async-start | bytes 2621440 | tf_op jit(solution)/shard_map/all_to_all | solution.py:287
  22.1 20.0 %all-to-all-done.1 = bf16[16,320,128]{2,1,0:T(8,128)(2,1)S(1)} async-done(((bf16[16,320,128]{2,1,0:T(8,128)(2,1)}), bf16[16,320,128]{2,1,0:T(8,128)(2,1)S(1)}, u32[]{:S(2)}, u32[]{:S(2)}) %all-to-all-start.1) | async-done | bytes 1310752 | tf_op jit(solution)/shard_map/all_to_all | solution.py:287
  42.1 0.0 copy-done.1
  42.1 0.0 copy-start
  42.1 2.0 %copy-done = bf16[128,13824]{1,0:T(8,128)(2,1)S(1)} copy-done((bf16[128,13824]{1,0:T(8,128)(2,1)S(1)}, bf16[128,13824]{1,0:T(8,128)(2,1)}, u32[]{:S(2)}) %copy-start) | copy-done | bytes 3538968
  44.1 14.7 %shard_map.86 = (bf16[2560,128]{1,0:T(8,128)(2,1)S(1)}, bf16[2560,128]{1,0:T(8,128)(2,1)S(1)}) custom-call(f32[1]{0:T(128)S(6)} %copy.9.teacher_ref, bf16[5120,128]{1,0:T(8,128)(2,1)S(1)} %bitcast.9, bf16[128,13824]{1,0:T(8,128)(2,1)S(1)} %copy-done, bf16[128,5120]{1,0:T(8,128)(2,1)S(1)} %copy-done.1), custom_call_target="tpu_custom_call" | custom-call | tf_op jit(solution)/shard_map/pallas_call | solution.py:266
  58.9 1.9 %collective-permute-start = (bf16[2560,128]{1,0:T(8,128)(2,1)S(1)}, bf16[2560,128]{1,0:T(8,128)(2,1)S(1)}, u32[]{:S(2)}, u32[]{:S(2)}) collective-permute-start(bf16[2560,128]{1,0:T(8,128)(2,1)S(1)} %get-tuple-element.6), channel_id=1, source_target_pairs={{0,1},{1,0},{2,3},{3,2},{4,5},{5,4},{6,7},{7,6},{8,9},{9,8},{10,11... | collective-permute-start | bytes 1966088 | tf_op jit(solution)/shard_map/ppermute | solution.py:308
  60.8 2.1 %collective-permute-done = bf16[2560,128]{1,0:T(8,128)(2,1)S(1)} collective-permute-done((bf16[2560,128]{1,0:T(8,128)(2,1)S(1)}, bf16[2560,128]{1,0:T(8,128)(2,1)S(1)}, u32[]{:S(2)}, u32[]{:S(2)}) %collective-permute-start) | collective-permute-done | bytes 655392 | tf_op jit(solution)/shard_map/ppermute | solution.py:308
  62.8 0.2 add_convert_fusion
  63.0 16.6 %all_to_all.48 = bf16[16,160,128]{2,1,0:T(8,128)(2,1)} all-to-all(bf16[16,160,128]{2,1,0:T(8,128)(2,1)S(1)} %bitcast.11), channel_id=1, replica_groups=mesh['zh'=4,'zl'=4,'x'=4,'y'=4,'c'=2] {'x','y'}, dimensions={0} | all-to-all | bytes 1310720 | tf_op jit(solution)/shard_map/all_to_all | solution.py:310
  79.6 1.8 %shard_map.87 = bf16[160,128]{1,0:T(8,128)(2,1)} custom-call(bf16[2560,128]{1,0:T(8,128)(2,1)} %bitcast.10), custom_call_target="tpu_custom_call" | custom-call | tf_op jit(solution)/shard_map/pallas_call | solution.py:266
  81.4 9.5 %all_to_all.49 = bf16[4,40,128]{2,1,0:T(8,128)(2,1)} all-to-all(bf16[4,40,128]{2,1,0:T(8,128)(2,1)} %bitcast.17), channel_id=1, replica_groups=mesh['zh'=4,'zl'=4,'x'=4,'y'=4,'c'=2] {'zl'}, dimensions={0} | all-to-all | bytes 81920 | tf_op jit(solution)/shard_map/all_to_all | solution.py:312
  90.9 1.4 %shard_map.88 = bf16[160,128]{1,0:T(8,128)(2,1)} custom-call(bf16[160,128]{1,0:T(8,128)(2,1)} %bitcast.15), custom_call_target="tpu_custom_call" | custom-call | tf_op jit(solution)/shard_map/pallas_call | solution.py:266
  92.3 25.8 %all_to_all.50 = bf16[4,40,128]{2,1,0:T(8,128)(2,1)} all-to-all(bf16[4,40,128]{2,1,0:T(8,128)(2,1)} %bitcast.16), channel_id=1, replica_groups=mesh['zh'=4,'zl'=4,'x'=4,'y'=4,'c'=2] {'zh'}, dimensions={0} | all-to-all | bytes 81920 | tf_op jit(solution)/shard_map/all_to_all | solution.py:314
  118.1 1.5 %shard_map.89 = (f32[32,108]{1,0:T(8,128)}, f32[32,40]{1,0:T(8,128)}, f32[1,40]{1,0:T(1,128)}) custom-call(bf16[160,128]{1,0:T(8,128)(2,1)} %bitcast.14), custom_call_target="tpu_custom_call" | custom-call | tf_op jit(solution)/shard_map/pallas_call | solution.py:266
Async XLA Ops:
  17.0 25.1 %copy-start.1 = (bf16[128,5120]{1,0:T(8,128)(2,1)S(1)}, bf16[128,5120]{1,0:T(8,128)(2,1)}, u32[]{:S(2)}) copy-start(bf16[128,5120]{1,0:T(8,128)(2,1)} %stream_hbm.1) | copy-start | bytes 3932164
  17.0 25.1 %all-to-all-start.1 = ((bf16[16,320,128]{2,1,0:T(8,128)(2,1)}), bf16[16,320,128]{2,1,0:T(8,128)(2,1)S(1)}, u32[]{:S(2)}, u32[]{:S(2)}) async-start(bf16[16,320,128]{2,1,0:T(8,128)(2,1)} %broadcast_in_dim.9), calls=%async_computation.1 | async-start | bytes 2621440 | tf_op jit(solution)/shard_map/all_to_all | solution.py:287
  42.1 2.0 %copy-start = (bf16[128,13824]{1,0:T(8,128)(2,1)S(1)}, bf16[128,13824]{1,0:T(8,128)(2,1)}, u32[]{:S(2)}) copy-start(bf16[128,13824]{1,0:T(8,128)(2,1)} %hidden_hbm.1) | copy-start | bytes 10616836
  58.9 4.0 %collective-permute-start = (bf16[2560,128]{1,0:T(8,128)(2,1)S(1)}, bf16[2560,128]{1,0:T(8,128)(2,1)S(1)}, u32[]{:S(2)}, u32[]{:S(2)}) collective-permute-start(bf16[2560,128]{1,0:T(8,128)(2,1)S(1)} %get-tuple-element.6), channel_id=1, source_target_pairs={{0,1},{1,0},{2,3},{3,2},{4,5},{5,4},{6,7},{7,6},{8,9},{9,8},{10,11... | collective-permute-start | bytes 1966088 | tf_op jit(solution)/shard_map/ppermute | solution.py:308

commit v2 on v0

v2 whole, which is shorter than its diff:
```python
import jax
import jax.numpy as jnp
from jax import lax
from jax.experimental import pallas as pl
from jax.experimental.pallas import tpu as pltpu
from jax.sharding import Mesh, PartitionSpec as P

QLEN = 32
PLEN = 48
TOK = QLEN + 2 * PLEN
D = 5120
FF = 13824
R = 32
NH = 4
NZ, NX, NY, NC = 4, 4, 4, 2
NXY = NX * NY
NK = NZ * NXY
WF = FF // (NK * NC)
WD = D // (NK * NC)
NG = WD // 8
FZ = FF // NZ
DZ = D // NZ
BLK = 48
LANE = 128
CH = NG * LANE
NCH = D // CH
DEV = ("zl", "x", "y", "c")
ALL = ("zh",) + DEV
SWAP = [(0, 1), (1, 0)]
f32 = jnp.float32
bf16 = jnp.bfloat16


def lanes(rows):
    return lax.broadcasted_iota(jnp.int32, (rows, LANE), 1)


def roll(value, shift):
    shift %= LANE
    return value if shift == 0 else pltpu.roll(value, shift, axis=1)


def dot(a, b):
    return jnp.dot(a, b, preferred_element_type=f32)


def dot_t(a, b):
    return lax.dot_general(a, b, (((1,), (1,)), ((), ())), preferred_element_type=f32)


def eye(n):
    i = lax.broadcasted_iota(jnp.int32, (n, n), 0)
    j = lax.broadcasted_iota(jnp.int32, (n, n), 1)
    return (i == j).astype(f32).astype(bf16)


def pack_kernel(a_ref, o_ref, g_ref, out_ref, a_s, o_s):
    a_s[...] = jnp.zeros_like(a_s)
    o_s[...] = jnp.zeros_like(o_s)
    a_s[:, :WF] = a_ref[...].astype(f32)
    o_s[:R, :WD] = o_ref[...].astype(f32)
    o_s[R : R + 1, :WD] = g_ref[...]
    t = o_s[...].T
    n = lanes(8)
    one = [t[8 * g : 8 * g + 8] for g in range(NG)]
    low = one[0]
    for g in range(1, 4):
        low = jnp.where(n < R * g, low, roll(one[g], R * g))
    high = one[4]
    for g in range(NG):
        high = jnp.where(n == R + g, roll(one[g], g), high)
    block = jnp.concatenate([a_s[...], low, high], axis=0).astype(bf16)
    for k in range(NZ):
        out_ref[k] = block


def stream_kernel(stream_ref, stream_out, perm):
    first = lax.axis_index("c") == 0
    n = lanes(1)
    row = lax.broadcasted_iota(jnp.int32, (DZ, LANE), 0)
    for own in range(NC):
        for g in range(NG):
            c = jnp.where(first, own, 1 - own)
            at = (n // 8) * (NC * WD) + n % 8 + c * WD + 8 * g
            t = own * NG + g
            perm[:, LANE * t : LANE * (t + 1)] = (row == at).astype(f32).astype(bf16)
    for z in range(NZ):
        cols = slice(DZ * z, DZ * (z + 1))
        stream_out[:, cols] = dot(stream_ref[:, cols], perm[...]).astype(bf16)


def hidden_kernel(hidden_ref, hidden_out):
    first = lax.axis_index("c") == 0
    inside = lanes(TOK) < WF
    for i in range(NXY):
        both = []
        for c in range(NC):
            t, s = divmod(WF * (NC * i + c), LANE)
            tile = hidden_ref[:, LANE * t : LANE * (t + 1)].astype(f32)
            if s + WF > LANE:
                nxt = hidden_ref[:, LANE * (t + 1) : LANE * (t + 2)].astype(f32)
                tile = jnp.where(lanes(TOK) >= s, tile, nxt)
            both.append(jnp.where(inside, roll(tile, -s), 0.0))
        cols = slice(LANE * i, LANE * (i + 1))
        hidden_out[0, 0, :, cols] = jnp.where(first, both[0], both[1]).astype(bf16)
        hidden_out[1, 0, :, cols] = jnp.where(first, both[1], both[0]).astype(bf16)


def main_kernel(
    teacher_ref, mine_ref, other_ref, hidden_hbm, stream_ref, keep_ref, send_ref,
    hidden, a_out, gain, unit, rows, grad_out, grad_gain, sems,
):
    blocks = (mine_ref, other_ref)
    copies = {}
    for own in range(NC):
        for z in range(NZ):
            copies[own, z] = pltpu.make_async_copy(
                hidden_hbm.at[own, z], hidden.at[own, z], sems.at[own * NZ + z]
            )
            copies[own, z].start()
    chunks = [(z, own) for z in range(NZ) for own in range(NC)]
    one = eye(LANE)
    k8 = 8

    for n, (z, own) in enumerate(chunks):
        x = blocks[own][:, z, R:, :].astype(f32)
        low = dot_t(one, x[:, :8].reshape(LANE, LANE).astype(bf16))
        high = dot_t(one, x[:, 8:].reshape(LANE, LANE).astype(bf16))
        for g in range(NG):
            cols = slice(CH * n + LANE * g, CH * n + LANE * (g + 1))
            a_out[:, cols] = (low[R * g : R * g + R] if g < 4 else high[:R]).astype(bf16)
            gain[:, cols] = jnp.broadcast_to(high[R + g : R + g + 1], (8, LANE))

    acc = jnp.zeros((TOK, R), f32)
    for own in range(NC):
        for k in range(0, NK, k8):
            z, i = divmod(k, NXY)
            if i == 0:
                copies[own, z].wait()
            a = jnp.concatenate([blocks[own][i + m, z, :R, :] for m in range(k8)], axis=1)
            acc = acc + dot_t(hidden[own, z, :, LANE * i : LANE * (i + k8)], a)
    low = acc.astype(bf16)
    low_t = dot_t(eye(R), low).astype(bf16)

    squares = jnp.zeros((TOK, LANE), f32)
    for n in range(NCH):
        cols = slice(CH * n, CH * (n + 1))
        s = stream_ref[:, cols].astype(f32) + dot(low, a_out[:, cols])
        unit[:, cols] = s
        for g in range(NG):
            x = s[:, LANE * g : LANE * (g + 1)]
            squares = squares + x * x
    inv = lax.rsqrt(jnp.sum(squares, axis=1, keepdims=True) / D + 1e-06)

    margin = jnp.zeros((1, CH), f32)
    acc = jnp.zeros((TOK, LANE), f32)
    for n in range(NCH):
        cols = slice(CH * n, CH * (n + 1))
        u = unit[:, cols] * inv
        unit[:, cols] = u
        gn = gain[:1, cols]
        uq = jnp.sum(u[:QLEN], axis=0, keepdims=True) / QLEN
        up = jnp.sum(u[QLEN : QLEN + PLEN], axis=0, keepdims=True) / PLEN
        un = jnp.sum(u[QLEN + PLEN :], axis=0, keepdims=True) / PLEN
        q = gn * uq
        pn = gn * (up - un)
        margin = margin + q * pn
        wq = pn * gn / QLEN
        wp = q * gn / PLEN
        rows[0:1, cols] = wq
        rows[1:2, cols] = wp
        rows[2:3, cols] = uq * pn
        prod = jnp.concatenate(
            [u[:QLEN] * wq, u[QLEN : QLEN + PLEN] * wp, u[QLEN + PLEN :] * -wp], axis=0
        )
        for g in range(NG):
            acc = acc + prod[:, LANE * g : LANE * (g + 1)]
    err = jnp.sum(margin, axis=1, keepdims=True) - teacher_ref[0]
    mean = jnp.sum(acc, axis=1, keepdims=True) / D
    scale = inv * err

    grad_gain[...] = jnp.zeros_like(grad_gain)
    acc = jnp.zeros((R, TOK), f32)
    for n in range(NCH):
        cols = slice(CH * n, CH * (n + 1))
        um = unit[:, cols] * mean
        wq = rows[0:1, cols]
        wp = rows[1:2, cols]
        d = jnp.concatenate(
            [wq - um[:QLEN], wp - um[QLEN : QLEN + PLEN], -wp - um[QLEN + PLEN :]], axis=0
        )
        d = (d * scale).astype(bf16)
        acc = acc + dot_t(a_out[:, cols], d)
        grad_out[:, cols] = dot(low_t, d).astype(bf16)
        gg = 2.0 * err * rows[2:3, cols]
        for g in range(NG):
            grad_gain[g : g + 1, LANE * n : LANE * (n + 1)] = gg[:, LANE * g : LANE * (g + 1)]
    d_low = acc.astype(bf16)

    outs = (keep_ref, send_ref)
    for own in (1, 0):
        for k in range(0, NK, k8):
            z, i = divmod(k, NXY)
            x = dot(d_low, hidden[own, z, :, LANE * i : LANE * (i + k8)]).astype(bf16)
            for m in range(k8):
                outs[own][i + m, z, :R, :] = x[:, LANE * m : LANE * (m + 1)]

    for n, (z, own) in enumerate(chunks):
        x = [grad_out[:, CH * n + LANE * g : CH * n + LANE * (g + 1)] for g in range(NG)]
        low = dot_t(one, jnp.concatenate(x[:4], axis=0))
        gg = grad_gain[:, LANE * n : LANE * (n + 1)].astype(bf16)
        zero = jnp.zeros((LANE - R - 16, LANE), bf16)
        high = dot_t(one, jnp.concatenate([x[4], gg, zero], axis=0))
        y = jnp.concatenate([low.reshape(NXY, 8, LANE), high.reshape(NXY, 8, LANE)], axis=1)
        outs[own][:, z, R:, :] = y.astype(bf16)


def final_kernel(in_ref, a_ref, o_ref, g_ref):
    b = jnp.sum(in_ref[...].astype(f32), axis=0)
    a_ref[...] = b[:R, :WF]
    low = b[R : R + 8]
    high = b[R + 8 :]
    n = lanes(8)
    parts = []
    for g in range(NG):
        part = roll(low, -R * g) if g < 4 else high
        parts.append(jnp.where(n == R, roll(high, -g), part))
    parts.append(jnp.zeros((LANE - 8 * NG, LANE), f32))
    t = jnp.concatenate(parts, axis=0).T
    o_ref[...] = t[:R, :WD]
    g_ref[...] = t[R : R + 1, :WD]


VMEM = pl.BlockSpec(memory_space=pltpu.VMEM)
SMEM = pl.BlockSpec(memory_space=pltpu.SMEM)


def call(kernel, shapes, *args, in_specs=None, out_specs=None, limit=None, **more):
    return pl.pallas_call(
        kernel,
        out_shape=shapes,
        in_specs=in_specs or [VMEM] * len(args),
        out_specs=out_specs or jax.tree.map(lambda _: VMEM, shapes),
        compiler_params=pltpu.CompilerParams(vmem_limit_bytes=limit) if limit else None,
        **more,
    )(*args)


def shape(*dims, dtype=bf16):
    return jax.ShapeDtypeStruct(dims, dtype)


def place_stream(stream):
    return call(
        stream_kernel, shape(TOK, D), stream,
        scratch_shapes=[pltpu.VMEM((DZ, DZ), bf16)],
        cost_estimate=pl.CostEstimate(flops=2 * TOK * D * DZ, bytes_accessed=4 * TOK * D, transcendentals=0),
        limit=16 * 2**20,
    )


def place_hidden(hidden):
    return call(
        hidden_kernel, shape(NC, NZ, TOK, NXY * LANE), hidden,
        grid=(NZ,),
        in_specs=[pl.BlockSpec((TOK, FZ), lambda z: (0, z))],
        out_specs=pl.BlockSpec((NC, 1, TOK, NXY * LANE), lambda z: (0, z, 0, 0)),
        cost_estimate=pl.CostEstimate(flops=TOK * FF * 8, bytes_accessed=6 * TOK * FF, transcendentals=0),
        limit=60 * 2**20,
    )


def local(teacher, mine, other, hidden, stream):
    return call(
        main_kernel, (shape(NXY, NZ, BLK, LANE), shape(NXY, NZ, BLK, LANE)), teacher, mine, other, hidden, stream,
        in_specs=[SMEM, VMEM, VMEM, pl.BlockSpec(memory_space=pl.ANY), VMEM],
        scratch_shapes=[
            pltpu.VMEM((NC, NZ, TOK, NXY * LANE), bf16),
            pltpu.VMEM((R, D), bf16),
            pltpu.VMEM((8, D), f32),
            pltpu.VMEM((TOK, D), f32),
            pltpu.VMEM((8, D), f32),
            pltpu.VMEM((R, D), bf16),
            pltpu.VMEM((16, NCH * LANE), f32),
            pltpu.SemaphoreType.DMA((NC * NZ,)),
        ],
        limit=46 * 2**20,
    )


def body(hidden, stream, adapter_in, adapter_out, norm_gain, teacher):
    mine = call(
        pack_kernel, shape(NZ, BLK, LANE), adapter_in, adapter_out, norm_gain,
        scratch_shapes=[pltpu.VMEM((R, LANE), f32), pltpu.VMEM((LANE, LANE), f32)],
    )
    column = lax.all_to_all(mine, "zl", 0, 0, tiled=True)
    column = column.reshape(1, NZ * BLK, LANE)
    copies = jnp.broadcast_to(column, (NXY, NZ * BLK, LANE))
    mine = lax.all_to_all(copies, ("x", "y"), 0, 0, tiled=True)
    mine, hidden, stream = lax.optimization_barrier(
        (mine, place_hidden(hidden), place_stream(stream))
    )
    mine = mine.reshape(NXY, NZ, BLK, LANE)
    other = lax.ppermute(mine, "c", SWAP)
    keep, send = local(teacher, mine, other, hidden, stream)
    other = lax.ppermute(send, "c", SWAP)
    pairs = (keep.astype(f32) + other.astype(f32)).astype(bf16)
    pairs = pairs.reshape(NXY, NZ * BLK, LANE)
    parts = lax.all_to_all(pairs, ("x", "y"), 0, 0, tiled=True)
    part = jnp.sum(parts.astype(f32), axis=0).astype(bf16)
    part = part.reshape(1, NZ, BLK, LANE)
    parts = jnp.broadcast_to(part, (NH, NZ, BLK, LANE)).reshape(NH * NZ, BLK, LANE)
    parts = lax.all_to_all(parts, ("zh", "zl"), 0, 0, tiled=True)
    shapes = (shape(R, WF, dtype=f32), shape(R, WD, dtype=f32), shape(1, WD, dtype=f32))
    return call(final_kernel, shapes, parts)


def solution(mesh):
    fine = Mesh(mesh.devices.reshape(NH, NZ, NX, NY, NC), ALL)
    return jax.shard_map(
        body,
        mesh=fine,
        in_specs=(P(ALL, None), P(ALL, None), P(None, DEV), P(None, DEV), P(None, DEV), P(ALL)),
        out_specs=(P(None, DEV), P(None, DEV), P(None, DEV)),
        check_vma=False,
    )
```

time: 2390 us -> 99.2 us (0.04)
  the two profiles are of different devices: /device:TPU:128 before, /device:TPU:32 now
where the time goes in v2:
time: 99.2 us; the launch traced here: 98.7 us
  blocking collectives  60.4 us (61%)
  Pallas kernels  19 us (19%)
  waiting for transfers between devices  8.31 us (8%)
  starting transfers between devices  8.26 us (8%)
  between operations  1.34 us (1%)
  local copies, waits for them, and re-layouts  1.06 us (1%)
    all_to_all x1, blocking collectives, body(): parts = lax.all_to_all(parts, ('zh', 'zl'), 0, 0, tiled=True)  29.4 us
    pallas_call x5, Pallas kernels, call(): pl.pallas_call(kernel, out_shape=shapes, in_specs=in_specs or [VMEM] * le...  19 us
    all_to_all x1, blocking collectives, body(): parts = lax.all_to_all(pairs, ('x', 'y'), 0, 0, tiled=True)  17.8 us
    all_to_all x1, blocking collectives, body(): column = lax.all_to_all(mine, 'zl', 0, 0, tiled=True)  13.2 us
    all_to_all x1, waiting for transfers between devices, body(): mine = lax.all_to_all(copies, ('x', 'y'), 0, 0, tiled=True)  4.58 us
    all_to_all x1, starting transfers between devices, body(): mine = lax.all_to_all(copies, ('x', 'y'), 0, 0, tiled=True)  4.31 us
    ppermute x1, waiting for transfers between devices, body(): other = lax.ppermute(send, 'c', SWAP)  2.13 us
    ppermute x1, starting transfers between devices, body(): other = lax.ppermute(send, 'c', SWAP)  2.04 us
  transfers between devices with their start and end apart: 3, of which 3 were waited for; matrix products, arithmetic and copies ran while one was open for 0% of the time, Pallas kernels for 8%

profile of v2, /device:TPU:32, one launch (start us, length us, event | category | flops | bytes accessed | tf_op | source)
XLA Modules:
  0.0 98.7 jit_solution(17287486014484462968)
XLA Ops:
  0.6 1.5 %shard_map.85 = bf16[4,48,128]{2,1,0:T(8,128)(2,1)} custom-call(bf16[32,108]{1,0:T(8,128)(2,1)} %a_ref.1, bf16[32,40]{1,0:T(8,128)(2,1)} %o_ref.1, f32[1,40]{1,0:T(1,128)} %g_ref.1), custom_call_target="tpu_custom_call" | custom-call | tf_op jit(solution)/shard_map/pallas_call | solution.py:239
  2.1 13.2 %all_to_all.20 = bf16[4,48,128]{2,1,0:T(8,128)(2,1)S(1)} all-to-all(bf16[4,48,128]{2,1,0:T(8,128)(2,1)} %shard_map.85), channel_id=1, replica_groups=mesh['zh'=4,'zl'=4,'x'=4,'y'=4,'c'=2] {'zl'}, dimensions={0} | all-to-all | bytes 98304 | tf_op jit(solution)/shard_map/all_to_all | solution.py:296
  15.3 1.0 %broadcast_in_dim.15 = bf16[16,192,128]{2,1,0:T(8,128)(2,1)} broadcast(bf16[192,128]{1,0:T(8,128)(2,1)S(1)} %bitcast.9), dimensions={1,2} | broadcast | bytes 835584 | tf_op jit(solution)/shard_map/broadcast_in_dim | solution.py:298
  16.4 4.3 %all-to-all-start.1 = ((bf16[16,192,128]{2,1,0:T(8,128)(2,1)}), bf16[16,192,128]{2,1,0:T(8,128)(2,1)S(1)}, u32[]{:S(2)}, u32[]{:S(2)}) async-start(bf16[16,192,128]{2,1,0:T(8,128)(2,1)} %broadcast_in_dim.15), calls=%async_computation.1 | async-start | bytes 1572864 | tf_op jit(solution)/shard_map/all_to_all | solution.py:299
  20.7 0.0 copy-start
  20.7 5.6 %shard_map.86.hidden_hbm = bf16[2,4,128,2048]{3,2,1,0:T(8,128)(2,1)} custom-call(bf16[128,13824]{1,0:T(8,128)(2,1)} %hidden_ref.1), custom_call_target="tpu_custom_call" | custom-call | flops 14155776 | bytes 10616832 | tf_op jit(solution)/shard_map/pallas_call | solution.py:239
  26.3 0.0 copy-done
  26.3 2.6 %shard_map.87.stream_ref = bf16[128,5120]{1,0:T(8,128)(2,1)S(1)} custom-call(bf16[128,5120]{1,0:T(8,128)(2,1)S(1)} %copy-done), custom_call_target="tpu_custom_call" | custom-call | flops 1677721600 | bytes 2621440 | tf_op jit(solution)/shard_map/pallas_call | solution.py:239
  29.0 4.6 %all-to-all-done.1 = bf16[16,192,128]{2,1,0:T(8,128)(2,1)S(1)} async-done(((bf16[16,192,128]{2,1,0:T(8,128)(2,1)}), bf16[16,192,128]{2,1,0:T(8,128)(2,1)S(1)}, u32[]{:S(2)}, u32[]{:S(2)}) %all-to-all-start.1) | async-done | bytes 786464 | tf_op jit(solution)/shard_map/all_to_all | solution.py:299
  33.6 1.9 %collective-permute-start = (bf16[16,4,48,128]{3,2,1,0:T(8,128)(2,1)S(1)}, bf16[16,4,48,128]{3,2,1,0:T(8,128)(2,1)S(1)}, u32[]{:S(2)}, u32[]{:S(2)}) collective-permute-start(bf16[16,4,48,128]{3,2,1,0:T(8,128)(2,1)S(1)} %bitcast.5), channel_id=1, source_target_pairs={{0,1},{1,0},{2,3},{3,2},{4,5},{5,4},{6,7},{7,6},{8,9},{9,8},{10,11... | collective-permute-start | bytes 2359304 | tf_op jit(solution)/shard_map/ppermute | solution.py:304
  36.1 1.6 %collective-permute-done.other_ref = bf16[16,4,48,128]{3,2,1,0:T(8,128)(2,1)S(1)} collective-permute-done((bf16[16,4,48,128]{3,2,1,0:T(8,128)(2,1)S(1)}, bf16[16,4,48,128]{3,2,1,0:T(8,128)(2,1)S(1)}, u32[]{:S(2)}, u32[]{:S(2)}) %collective-permute-start) | collective-permute-done | bytes 786464 | tf_op jit(solution)/shard_map/ppermute | solution.py:304
  37.7 7.5 %shard_map.88 = (bf16[16,4,48,128]{3,2,1,0:T(8,128)(2,1)S(1)}, bf16[16,4,48,128]{3,2,1,0:T(8,128)(2,1)S(1)}) custom-call(f32[1]{0:T(128)S(6)} %copy.9.teacher_ref, bf16[16,4,48,128]{3,2,1,0:T(8,128)(2,1)S(1)} %bitcast.6, bf16[16,4,48,128]{3,2,1,0:T(8,128)(2,1)S(1)} %collective-permute-done.other_ref, bf16[2,4,128,2048]{3,2,1,0:T(8,128)(2,1)} %shard_map.86.hidden_hbm, ...), custom_call_target="tpu_custom_call" | custom-call | tf_op jit(solution)/shard_map/pallas_call | solution.py:239
  45.2 2.0 %collective-permute-start.1 = (bf16[16,4,48,128]{3,2,1,0:T(8,128)(2,1)S(1)}, bf16[16,4,48,128]{3,2,1,0:T(8,128)(2,1)S(1)}, u32[]{:S(2)}, u32[]{:S(2)}) collective-permute-start(bf16[16,4,48,128]{3,2,1,0:T(8,128)(2,1)S(1)} %get-tuple-element.12), channel_id=1, source_target_pairs={{0,1},{1,0},{2,3},{3,2},{4,5},{5,4},{6,7},{7,6},{8,9},{9,8},{10,11... | collective-permute-start | bytes 2359304 | tf_op jit(solution)/shard_map/ppermute | solution.py:306
  47.3 2.1 %collective-permute-done.1 = bf16[16,4,48,128]{3,2,1,0:T(8,128)(2,1)S(1)} collective-permute-done((bf16[16,4,48,128]{3,2,1,0:T(8,128)(2,1)S(1)}, bf16[16,4,48,128]{3,2,1,0:T(8,128)(2,1)S(1)}, u32[]{:S(2)}, u32[]{:S(2)}) %collective-permute-start.1) | collective-permute-done | bytes 786464 | tf_op jit(solution)/shard_map/ppermute | solution.py:306
  49.4 0.2 add_convert_fusion
  49.6 17.8 %all_to_all.21 = bf16[16,192,128]{2,1,0:T(8,128)(2,1)S(1)} all-to-all(bf16[16,192,128]{2,1,0:T(8,128)(2,1)S(1)} %bitcast.7), channel_id=1, replica_groups=mesh['zh'=4,'zl'=4,'x'=4,'y'=4,'c'=2] {'x','y'}, dimensions={0} | all-to-all | bytes 1572864 | tf_op jit(solution)/shard_map/all_to_all | solution.py:309
  67.5 0.1 reduce_sum.12
  67.6 29.4 %all_to_all.22.in_ref = bf16[16,48,128]{2,1,0:T(8,128)(2,1)} all-to-all(bf16[16,48,128]{2,1,0:T(8,128)(2,1)S(1)} %bitcast.8), channel_id=1, replica_groups=mesh['zh'=4,'zl'=4,'x'=4,'y'=4,'c'=2] {'zh','zl'}, dimensions={0} | all-to-all | bytes 393216 | tf_op jit(solution)/shard_map/all_to_all | solution.py:313
  97.0 1.7 %shard_map.89 = (f32[32,108]{1,0:T(8,128)}, f32[32,40]{1,0:T(8,128)}, f32[1,40]{1,0:T(1,128)}) custom-call(bf16[16,48,128]{2,1,0:T(8,128)(2,1)} %all_to_all.22.in_ref), custom_call_target="tpu_custom_call" | custom-call | tf_op jit(solution)/shard_map/pallas_call | solution.py:239
  (1 shorter events, 0.0 us)
Async XLA Ops:
  16.4 17.2 %all-to-all-start.1 = ((bf16[16,192,128]{2,1,0:T(8,128)(2,1)}), bf16[16,192,128]{2,1,0:T(8,128)(2,1)S(1)}, u32[]{:S(2)}, u32[]{:S(2)}) async-start(bf16[16,192,128]{2,1,0:T(8,128)(2,1)} %broadcast_in_dim.15), calls=%async_computation.1 | async-start | bytes 1572864 | tf_op jit(solution)/shard_map/all_to_all | solution.py:299
  20.7 5.6 %copy-start = (bf16[128,5120]{1,0:T(8,128)(2,1)S(1)}, bf16[128,5120]{1,0:T(8,128)(2,1)}, u32[]{:S(2)}) copy-start(bf16[128,5120]{1,0:T(8,128)(2,1)} %stream_ref.1) | copy-start | bytes 3932164
  33.6 4.2 %collective-permute-start = (bf16[16,4,48,128]{3,2,1,0:T(8,128)(2,1)S(1)}, bf16[16,4,48,128]{3,2,1,0:T(8,128)(2,1)S(1)}, u32[]{:S(2)}, u32[]{:S(2)}) collective-permute-start(bf16[16,4,48,128]{3,2,1,0:T(8,128)(2,1)S(1)} %bitcast.5), channel_id=1, source_target_pairs={{0,1},{1,0},{2,3},{3,2},{4,5},{5,4},{6,7},{7,6},{8,9},{9,8},{10,11... | collective-permute-start | bytes 2359304 | tf_op jit(solution)/shard_map/ppermute | solution.py:304
  45.2 4.2 %collective-permute-start.1 = (bf16[16,4,48,128]{3,2,1,0:T(8,128)(2,1)S(1)}, bf16[16,4,48,128]{3,2,1,0:T(8,128)(2,1)S(1)}, u32[]{:S(2)}, u32[]{:S(2)}) collective-permute-start(bf16[16,4,48,128]{3,2,1,0:T(8,128)(2,1)S(1)} %get-tuple-element.12), channel_id=1, source_target_pairs={{0,1},{1,0},{2,3},{3,2},{4,5},{5,4},{6,7},{7,6},{8,9},{9,8},{10,11... | collective-permute-start | bytes 2359304 | tf_op jit(solution)/shard_map/ppermute | solution.py:306

commit v3 on v2

--- a/solution.py
+++ b/solution.py
@@ -20,8 +20,11 @@
 NG = WD // 8
 FZ = FF // NZ
 DZ = D // NZ
-BLK = 48
+BLK = 40
 LANE = 128
+LAST = 108
+GAIN = 116
+TOP = NZ * R
 CH = NG * LANE
 NCH = D // CH
 DEV = ("zl", "x", "y", "c")
@@ -60,16 +63,18 @@
     a_s[:, :WF] = a_ref[...].astype(f32)
     o_s[:R, :WD] = o_ref[...].astype(f32)
     o_s[R : R + 1, :WD] = g_ref[...]
-    t = o_s[...].T
+    o = o_s[...]
+    t = o.T
+    one = [t[8 * g : 8 * g + 8] for g in range(NG)]
+    n = lanes(R)
+    top = jnp.where(n < LAST, a_s[...], jnp.where(n < GAIN, roll(o[:R], LAST - R), 0.0))
     n = lanes(8)
-    one = [t[8 * g : 8 * g + 8] for g in range(NG)]
-    low = one[0]
+    low, gains = one[0], top[:8]
     for g in range(1, 4):
         low = jnp.where(n < R * g, low, roll(one[g], R * g))
-    high = one[4]
     for g in range(NG):
-        high = jnp.where(n == R + g, roll(one[g], g), high)
-    block = jnp.concatenate([a_s[...], low, high], axis=0).astype(bf16)
+        gains = jnp.where(n == GAIN + g, roll(one[g], GAIN + g - R), gains)
+    block = jnp.concatenate([gains, top[8:], low], axis=0).astype(bf16)
     for k in range(NZ):
         out_ref[k] = block
 
@@ -90,20 +95,20 @@
 
 
 def hidden_kernel(hidden_ref, hidden_out):
-    first = lax.axis_index("c") == 0
+    core = lax.axis_index("c")
     inside = lanes(TOK) < WF
-    for i in range(NXY):
-        both = []
-        for c in range(NC):
-            t, s = divmod(WF * (NC * i + c), LANE)
-            tile = hidden_ref[:, LANE * t : LANE * (t + 1)].astype(f32)
-            if s + WF > LANE:
-                nxt = hidden_ref[:, LANE * (t + 1) : LANE * (t + 2)].astype(f32)
-                tile = jnp.where(lanes(TOK) >= s, tile, nxt)
-            both.append(jnp.where(inside, roll(tile, -s), 0.0))
-        cols = slice(LANE * i, LANE * (i + 1))
-        hidden_out[0, 0, :, cols] = jnp.where(first, both[0], both[1]).astype(bf16)
-        hidden_out[1, 0, :, cols] = jnp.where(first, both[1], both[0]).astype(bf16)
+    now, tile = -1, None
+    for n in range(NXY * NC):
+        t, s = divmod(WF * n, LANE)
+        if t != now:
+            now, tile = t, hidden_ref[:, LANE * t : LANE * (t + 1)].astype(f32)
+        x = tile
+        if s + WF > LANE:
+            now, tile = t + 1, hidden_ref[:, LANE * (t + 1) : LANE * (t + 2)].astype(f32)
+            x = jnp.where(lanes(TOK) >= s, x, tile)
+        x = jnp.where(inside, roll(x, -s), 0.0).astype(bf16)
+        own = core if n % NC == 0 else 1 - core
+        hidden_out[own, 0, :, LANE * (n // NC) : LANE * (n // NC + 1)] = x
 
 
 def main_kernel(
@@ -111,6 +116,12 @@
     hidden, a_out, gain, unit, rows, grad_out, grad_gain, sems,
 ):
     blocks = (mine_ref, other_ref)
+    one = eye(LANE)
+    k8 = 8
+    n = NXY * LANE
+    spread = lax.broadcasted_iota(jnp.int32, (LANE, n), 0)
+    spread = spread // 8 * LANE + spread % 8 + LAST
+    spread = (spread == lax.broadcasted_iota(jnp.int32, (LANE, n), 1)).astype(f32).astype(bf16)
     copies = {}
     for own in range(NC):
         for z in range(NZ):
@@ -118,18 +129,28 @@
                 hidden_hbm.at[own, z], hidden.at[own, z], sems.at[own * NZ + z]
             )
             copies[own, z].start()
-    chunks = [(z, own) for z in range(NZ) for own in range(NC)]
     one = eye(LANE)
     k8 = 8
 
-    for n, (z, own) in enumerate(chunks):
-        x = blocks[own][:, z, R:, :].astype(f32)
-        low = dot_t(one, x[:, :8].reshape(LANE, LANE).astype(bf16))
-        high = dot_t(one, x[:, 8:].reshape(LANE, LANE).astype(bf16))
-        for g in range(NG):
-            cols = slice(CH * n + LANE * g, CH * n + LANE * (g + 1))
-            a_out[:, cols] = (low[R * g : R * g + R] if g < 4 else high[:R]).astype(bf16)
-            gain[:, cols] = jnp.broadcast_to(high[R + g : R + g + 1], (8, LANE))
+    for own in range(NC):
+        top = [
+            jnp.concatenate([blocks[own][i, R * z : R * (z + 1), :] for i in range(NXY)], axis=1)
+            for z in range(NZ)
+        ]
+        last = dot_t(jnp.concatenate(top, axis=0), spread)
+        low = blocks[own][:, TOP:, :].astype(f32)
+        for z in range(NZ):
+            n = CH * (NC * z + own)
+            x = low[:, 8 * z : 8 * z + 8].reshape(LANE, LANE).astype(bf16)
+            x = dot_t(one, x)
+            y = blocks[own][:, R * z : R * z + 16, :].astype(f32)
+            y = dot_t(one[LANE - 16 :], y[:, :8].reshape(LANE, LANE).astype(bf16))
+            for g in range(NG):
+                cols = slice(n + LANE * g, n + LANE * (g + 1))
+                part = x[R * g : R * g + R] if g < 4 else last[R * z : R * z + R]
+                a_out[:, cols] = part.astype(bf16)
+                row = GAIN - LANE + 16 + g
+                gain[:, cols] = jnp.broadcast_to(y[row : row + 1], (8, LANE))
 
     acc = jnp.zeros((TOK, R), f32)
     for own in range(NC):
@@ -137,7 +158,8 @@
             z, i = divmod(k, NXY)
             if i == 0:
                 copies[own, z].wait()
-            a = jnp.concatenate([blocks[own][i + m, z, :R, :] for m in range(k8)], axis=1)
+            a = [blocks[own][i + m, R * z : R * (z + 1), :] for m in range(k8)]
+            a = jnp.concatenate(a, axis=1)
             acc = acc + dot_t(hidden[own, z, :, LANE * i : LANE * (i + k8)], a)
     low = acc.astype(bf16)
     low_t = dot_t(eye(R), low).astype(bf16)
@@ -194,40 +216,45 @@
         grad_out[:, cols] = dot(low_t, d).astype(bf16)
         gg = 2.0 * err * rows[2:3, cols]
         for g in range(NG):
-            grad_gain[g : g + 1, LANE * n : LANE * (n + 1)] = gg[:, LANE * g : LANE * (g + 1)]
+            row = GAIN - LANE + 16 + g
+            grad_gain[row : row + 1, LANE * n : LANE * (n + 1)] = gg[:, LANE * g : LANE * (g + 1)]
     d_low = acc.astype(bf16)
 
     outs = (keep_ref, send_ref)
     for own in (1, 0):
-        for k in range(0, NK, k8):
-            z, i = divmod(k, NXY)
-            x = dot(d_low, hidden[own, z, :, LANE * i : LANE * (i + k8)]).astype(bf16)
-            for m in range(k8):
-                outs[own][i + m, z, :R, :] = x[:, LANE * m : LANE * (m + 1)]
-
-    for n, (z, own) in enumerate(chunks):
-        x = [grad_out[:, CH * n + LANE * g : CH * n + LANE * (g + 1)] for g in range(NG)]
-        low = dot_t(one, jnp.concatenate(x[:4], axis=0))
-        gg = grad_gain[:, LANE * n : LANE * (n + 1)].astype(bf16)
-        zero = jnp.zeros((LANE - R - 16, LANE), bf16)
-        high = dot_t(one, jnp.concatenate([x[4], gg, zero], axis=0))
-        y = jnp.concatenate([low.reshape(NXY, 8, LANE), high.reshape(NXY, 8, LANE)], axis=1)
-        outs[own][:, z, R:, :] = y.astype(bf16)
+        low = []
+        last = [CH * (NC * z + own) + LANE * (NG - 1) for z in range(NZ)]
+        last = jnp.concatenate([grad_out[:, n : n + LANE] for n in last], axis=0)
+        last = dot(last, spread)
+        for z in range(NZ):
+            n = NC * z + own
+            x = [grad_out[:, CH * n + LANE * g : CH * n + LANE * (g + 1)] for g in range(4)]
+            y = dot_t(one, jnp.concatenate(x, axis=0))
+            low.append(y.reshape(NXY, 8, LANE))
+            gg = grad_gain[:, LANE * n : LANE * (n + 1)].astype(bf16)
+            gg = dot_t(one, jnp.concatenate([jnp.zeros((LANE - 16, LANE), bf16), gg], axis=0))
+            for i in range(0, NXY, k8):
+                cols = slice(LANE * i, LANE * (i + k8))
+                top = dot(d_low, hidden[own, z, :, cols]) + last[R * z : R * (z + 1), cols]
+                for m in range(k8):
+                    t = top[:, LANE * m : LANE * (m + 1)]
+                    t = jnp.concatenate([t[:8] + gg[8 * (i + m) : 8 * (i + m) + 8], t[8:]], axis=0)
+                    outs[own][i + m, R * z : R * (z + 1), :] = t.astype(bf16)
+        outs[own][:, TOP:, :] = jnp.concatenate(low, axis=1).astype(bf16)
 
 
 def final_kernel(in_ref, a_ref, o_ref, g_ref):
-    b = jnp.sum(in_ref[...].astype(f32), axis=0)
+    b = in_ref[...]
     a_ref[...] = b[:R, :WF]
-    low = b[R : R + 8]
-    high = b[R + 8 :]
+    low = b[R:]
     n = lanes(8)
     parts = []
     for g in range(NG):
-        part = roll(low, -R * g) if g < 4 else high
-        parts.append(jnp.where(n == R, roll(high, -g), part))
+        part = roll(low, -R * g) if g < 4 else low
+        parts.append(jnp.where(n == R, roll(b[:8], R - GAIN - g), part))
     parts.append(jnp.zeros((LANE - 8 * NG, LANE), f32))
     t = jnp.concatenate(parts, axis=0).T
-    o_ref[...] = t[:R, :WD]
+    o_ref[...] = jnp.where(lanes(R) < R, t[:R], roll(b[:R], R - LAST))[:, :WD]
     g_ref[...] = t[R : R + 1, :WD]
 
 
@@ -272,7 +299,7 @@
 
 def local(teacher, mine, other, hidden, stream):
     return call(
-        main_kernel, (shape(NXY, NZ, BLK, LANE), shape(NXY, NZ, BLK, LANE)), teacher, mine, other, hidden, stream,
+        main_kernel, (shape(NXY, NZ * BLK, LANE), shape(NXY, NZ * BLK, LANE)), teacher, mine, other, hidden, stream,
         in_specs=[SMEM, VMEM, VMEM, pl.BlockSpec(memory_space=pl.ANY), VMEM],
         scratch_shapes=[
             pltpu.VMEM((NC, NZ, TOK, NXY * LANE), bf16),
@@ -284,7 +311,7 @@
             pltpu.VMEM((16, NCH * LANE), f32),
             pltpu.SemaphoreType.DMA((NC * NZ,)),
         ],
-        limit=46 * 2**20,
+        limit=49 * 2**20,
     )
 
 
@@ -294,25 +321,26 @@
         scratch_shapes=[pltpu.VMEM((R, LANE), f32), pltpu.VMEM((LANE, LANE), f32)],
     )
     column = lax.all_to_all(mine, "zl", 0, 0, tiled=True)
-    column = column.reshape(1, NZ * BLK, LANE)
+    column, stream = lax.optimization_barrier((column, place_stream(stream)))
+    column = jnp.concatenate(
+        [column[:, :R].reshape(1, TOP, LANE), column[:, R:].reshape(1, 8 * NZ, LANE)], axis=1
+    )
     copies = jnp.broadcast_to(column, (NXY, NZ * BLK, LANE))
     mine = lax.all_to_all(copies, ("x", "y"), 0, 0, tiled=True)
-    mine, hidden, stream = lax.optimization_barrier(
-        (mine, place_hidden(hidden), place_stream(stream))
-    )
-    mine = mine.reshape(NXY, NZ, BLK, LANE)
+    mine, hidden = lax.optimization_barrier((mine, place_hidden(hidden)))
     other = lax.ppermute(mine, "c", SWAP)
     keep, send = local(teacher, mine, other, hidden, stream)
     other = lax.ppermute(send, "c", SWAP)
     pairs = (keep.astype(f32) + other.astype(f32)).astype(bf16)
-    pairs = pairs.reshape(NXY, NZ * BLK, LANE)
     parts = lax.all_to_all(pairs, ("x", "y"), 0, 0, tiled=True)
     part = jnp.sum(parts.astype(f32), axis=0).astype(bf16)
-    part = part.reshape(1, NZ, BLK, LANE)
+    part = jnp.concatenate(
+        [part[:TOP].reshape(1, NZ, R, LANE), part[TOP:].reshape(1, NZ, 8, LANE)], axis=2
+    )
     parts = jnp.broadcast_to(part, (NH, NZ, BLK, LANE)).reshape(NH * NZ, BLK, LANE)
     parts = lax.all_to_all(parts, ("zh", "zl"), 0, 0, tiled=True)
     shapes = (shape(R, WF, dtype=f32), shape(R, WD, dtype=f32), shape(1, WD, dtype=f32))
-    return call(final_kernel, shapes, parts)
+    return call(final_kernel, shapes, jnp.sum(parts.astype(f32), axis=0))
 
 
 def solution(mesh):

time: 99.2 us -> 94.9 us (0.957)
  blocking collectives: 60.4 us -> 43.7 us
  starting transfers between devices: 8.26 us -> 17 us
  waiting for transfers between devices: 8.31 us -> 10.5 us
  local copies, waits for them, and re-layouts: 1.06 us -> 2.28 us
    all_to_all x1 -> x0, blocking collectives: 13.2 us -> none  [body(): column = lax.all_to_all(mine, 'zl', 0, 0, tiled=True)]
    all_to_all x0 -> x1, starting transfers between devices: none -> 8.72 us  [body(): column = lax.all_to_all(mine, 'zl', 0, 0, tiled=True)]
    all_to_all x1, waiting for transfers between devices: 4.58 us -> 6.61 us  [body(): mine = lax.all_to_all(copies, ('x', 'y'), 0, 0, tiled=True)]
    all_to_all x1, blocking collectives: 29.4 us -> 27.4 us  [body(): parts = lax.all_to_all(parts, ('zh', 'zl'), 0, 0, tiled=True)]
    all_to_all x1, blocking collectives: 17.8 us -> 16.3 us  [body(): parts = lax.all_to_all(pairs, ('x', 'y'), 0, 0, tiled=True)]
    unnamed x2, local copies, waits for them, and re-layouts: 0.01 us -> 1.32 us
  transfers between devices with their start and end apart: 3 -> 4, of which waited for: 3 -> 4; matrix products, arithmetic and copies ran while one was open for 0% -> 0% of each run, Pallas kernels for 8% -> 8%
where the time goes in v3:
time: 94.9 us; the launch traced here: 94.3 us
  blocking collectives  43.7 us (46%)
  Pallas kernels  18.6 us (20%)
  starting transfers between devices  17 us (18%)
  waiting for transfers between devices  10.5 us (11%)
  local copies, waits for them, and re-layouts  2.28 us (2%)
  between operations  1.36 us (1%)
    all_to_all x1, blocking collectives, body(): parts = lax.all_to_all(parts, ('zh', 'zl'), 0, 0, tiled=True)  27.4 us
    pallas_call x5, Pallas kernels, call(): pl.pallas_call(kernel, out_shape=shapes, in_specs=in_specs or [VMEM] * le...  18.6 us
    all_to_all x1, blocking collectives, body(): parts = lax.all_to_all(pairs, ('x', 'y'), 0, 0, tiled=True)  16.3 us
    all_to_all x1, starting transfers between devices, body(): column = lax.all_to_all(mine, 'zl', 0, 0, tiled=True)  8.72 us
    all_to_all x1, waiting for transfers between devices, body(): mine = lax.all_to_all(copies, ('x', 'y'), 0, 0, tiled=True)  6.61 us
    all_to_all x1, starting transfers between devices, body(): mine = lax.all_to_all(copies, ('x', 'y'), 0, 0, tiled=True)  4.31 us
    ppermute x1, starting transfers between devices, body(): other = lax.ppermute(send, 'c', SWAP)  2.05 us
    ppermute x1, waiting for transfers between devices, body(): other = lax.ppermute(send, 'c', SWAP)  1.94 us
  transfers between devices with their start and end apart: 4, of which 4 were waited for; matrix products, arithmetic and copies ran while one was open for 0% of the time, Pallas kernels for 8%

profile of v3, /device:TPU:32, one launch (start us, length us, event | category | flops | bytes accessed | tf_op | source)
XLA Modules:
  0.0 94.3 jit_solution(14076028331104201520)
XLA Ops:
  0.6 1.5 %shard_map.85 = bf16[4,40,128]{2,1,0:T(8,128)(2,1)} custom-call(bf16[32,108]{1,0:T(8,128)(2,1)} %a_ref.1, bf16[32,40]{1,0:T(8,128)(2,1)} %o_ref.1, f32[1,40]{1,0:T(1,128)} %g_ref.1), custom_call_target="tpu_custom_call" | custom-call | tf_op jit(solution)/shard_map/pallas_call | solution.py:266
  2.1 8.7 %all-to-all-start = ((bf16[4,40,128]{2,1,0:T(8,128)(2,1)}), bf16[4,40,128]{2,1,0:T(8,128)(2,1)S(1)}, u32[]{:S(2)}, u32[]{:S(2)}) async-start(bf16[4,40,128]{2,1,0:T(8,128)(2,1)} %shard_map.85), calls=%async_computation | async-start | bytes 81920 | tf_op jit(solution)/shard_map/all_to_all | solution.py:323
  10.8 0.0 copy-start
  10.8 1.3 %copy-done = bf16[128,5120]{1,0:T(8,128)(2,1)S(1)} copy-done((bf16[128,5120]{1,0:T(8,128)(2,1)S(1)}, bf16[128,5120]{1,0:T(8,128)(2,1)}, u32[]{:S(2)}) %copy-start) | copy-done | bytes 1310744
  12.2 2.6 %shard_map.86.stream_ref = bf16[128,5120]{1,0:T(8,128)(2,1)S(1)} custom-call(bf16[128,5120]{1,0:T(8,128)(2,1)S(1)} %copy-done), custom_call_target="tpu_custom_call" | custom-call | flops 1677721600 | bytes 2621440 | tf_op jit(solution)/shard_map/pallas_call | solution.py:266
  14.8 0.5 all-to-all-done
  15.3 0.9 broadcast_in_dim.15
  16.2 4.3 %all-to-all-start.1 = ((bf16[16,160,128]{2,1,0:T(8,128)(2,1)}), bf16[16,160,128]{2,1,0:T(8,128)(2,1)S(1)}, u32[]{:S(2)}, u32[]{:S(2)}) async-start(bf16[16,160,128]{2,1,0:T(8,128)(2,1)} %broadcast_in_dim.15), calls=%async_computation.1 | async-start | bytes 1310720 | tf_op jit(solution)/shard_map/all_to_all | solution.py:329
  20.5 5.3 %shard_map.87.hidden_hbm = bf16[2,4,128,2048]{3,2,1,0:T(8,128)(2,1)} custom-call(bf16[128,13824]{1,0:T(8,128)(2,1)} %hidden_ref.1), custom_call_target="tpu_custom_call" | custom-call | flops 14155776 | bytes 10616832 | tf_op jit(solution)/shard_map/pallas_call | solution.py:266
  25.8 6.6 %all-to-all-done.1.mine_ref = bf16[16,160,128]{2,1,0:T(8,128)(2,1)S(1)} async-done(((bf16[16,160,128]{2,1,0:T(8,128)(2,1)}), bf16[16,160,128]{2,1,0:T(8,128)(2,1)S(1)}, u32[]{:S(2)}, u32[]{:S(2)}) %all-to-all-start.1) | async-done | bytes 655392 | tf_op jit(solution)/shard_map/all_to_all | solution.py:329
  32.4 1.9 %collective-permute-start = (bf16[16,160,128]{2,1,0:T(8,128)(2,1)S(1)}, bf16[16,160,128]{2,1,0:T(8,128)(2,1)S(1)}, u32[]{:S(2)}, u32[]{:S(2)}) collective-permute-start(bf16[16,160,128]{2,1,0:T(8,128)(2,1)S(1)} %all-to-all-done.1.mine_ref), channel_id=1, source_target_pairs={{0,1},{1,0},{2,3},{3,2},{4,5},{5,4},{6,7},{7,6},{8,9},{9,8},{10,11... | collective-permute-start | bytes 1966088 | tf_op jit(solution)/shard_map/ppermute | solution.py:331
  35.0 1.4 %collective-permute-done.other_ref = bf16[16,160,128]{2,1,0:T(8,128)(2,1)S(1)} collective-permute-done((bf16[16,160,128]{2,1,0:T(8,128)(2,1)S(1)}, bf16[16,160,128]{2,1,0:T(8,128)(2,1)S(1)}, u32[]{:S(2)}, u32[]{:S(2)}) %collective-permute-start) | collective-permute-done | bytes 655392 | tf_op jit(solution)/shard_map/ppermute | solution.py:331
  36.4 7.8 %shard_map.88 = (bf16[16,160,128]{2,1,0:T(8,128)(2,1)S(1)}, bf16[16,160,128]{2,1,0:T(8,128)(2,1)S(1)}) custom-call(f32[1]{0:T(128)S(6)} %copy.9.teacher_ref, bf16[16,160,128]{2,1,0:T(8,128)(2,1)S(1)} %all-to-all-done.1.mine_ref, bf16[16,160,128]{2,1,0:T(8,128)(2,1)S(1)} %collective-permute-done.other_ref, bf16[2,4,128,2048]{3,2,1,0:T(8,128)(2,1)} %shard_map.87.hidden_hbm, ...), custom_call_target="tpu_custom_call" | custom-call | tf_op jit(solution)/shard_map/pallas_call | solution.py:266
  44.2 2.0 %collective-permute-start.1 = (bf16[16,160,128]{2,1,0:T(8,128)(2,1)S(1)}, bf16[16,160,128]{2,1,0:T(8,128)(2,1)S(1)}, u32[]{:S(2)}, u32[]{:S(2)}) collective-permute-start(bf16[16,160,128]{2,1,0:T(8,128)(2,1)S(1)} %get-tuple-element.14), channel_id=1, source_target_pairs={{0,1},{1,0},{2,3},{3,2},{4,5},{5,4},{6,7},{7,6},{8,9},{9,8},{10,11... | collective-permute-start | bytes 1966088 | tf_op jit(solution)/shard_map/ppermute | solution.py:333
  46.2 1.9 %collective-permute-done.1 = bf16[16,160,128]{2,1,0:T(8,128)(2,1)S(1)} collective-permute-done((bf16[16,160,128]{2,1,0:T(8,128)(2,1)S(1)}, bf16[16,160,128]{2,1,0:T(8,128)(2,1)S(1)}, u32[]{:S(2)}, u32[]{:S(2)}) %collective-permute-start.1) | collective-permute-done | bytes 655392 | tf_op jit(solution)/shard_map/ppermute | solution.py:333
  48.2 0.2 add_convert_fusion
  48.3 16.3 %all_to_all.20 = bf16[16,160,128]{2,1,0:T(8,128)(2,1)S(1)} all-to-all(bf16[16,160,128]{2,1,0:T(8,128)(2,1)S(1)} %add_convert_fusion), channel_id=1, replica_groups=mesh['zh'=4,'zl'=4,'x'=4,'y'=4,'c'=2] {'x','y'}, dimensions={0} | all-to-all | bytes 1310720 | tf_op jit(solution)/shard_map/all_to_all | solution.py:335
  64.7 0.1 reduce_sum.21
  64.8 27.4 %all_to_all.21 = bf16[16,40,128]{2,1,0:T(8,128)(2,1)S(1)} all-to-all(bf16[16,40,128]{2,1,0:T(8,128)(2,1)S(1)} %bitcast.11), channel_id=1, replica_groups=mesh['zh'=4,'zl'=4,'x'=4,'y'=4,'c'=2] {'zh','zl'}, dimensions={0} | all-to-all | bytes 327680 | tf_op jit(solution)/shard_map/all_to_all | solution.py:341
  92.2 0.6 convert_reduce_fusion.in_ref
  92.8 1.5 %shard_map.89 = (f32[32,108]{1,0:T(8,128)}, f32[32,40]{1,0:T(8,128)}, f32[1,40]{1,0:T(1,128)}) custom-call(f32[40,128]{1,0:T(8,128)} %convert_reduce_fusion.in_ref), custom_call_target="tpu_custom_call" | custom-call | tf_op jit(solution)/shard_map/pallas_call | solution.py:266
  (7 shorter events, 0.1 us)
Async XLA Ops:
  2.1 13.2 %all-to-all-start = ((bf16[4,40,128]{2,1,0:T(8,128)(2,1)}), bf16[4,40,128]{2,1,0:T(8,128)(2,1)S(1)}, u32[]{:S(2)}, u32[]{:S(2)}) async-start(bf16[4,40,128]{2,1,0:T(8,128)(2,1)} %shard_map.85), calls=%async_computation | async-start | bytes 81920 | tf_op jit(solution)/shard_map/all_to_all | solution.py:323
  10.8 1.3 %copy-start = (bf16[128,5120]{1,0:T(8,128)(2,1)S(1)}, bf16[128,5120]{1,0:T(8,128)(2,1)}, u32[]{:S(2)}) copy-start(bf16[128,5120]{1,0:T(8,128)(2,1)} %stream_ref.1) | copy-start | bytes 3932164
  16.2 16.2 %all-to-all-start.1 = ((bf16[16,160,128]{2,1,0:T(8,128)(2,1)}), bf16[16,160,128]{2,1,0:T(8,128)(2,1)S(1)}, u32[]{:S(2)}, u32[]{:S(2)}) async-start(bf16[16,160,128]{2,1,0:T(8,128)(2,1)} %broadcast_in_dim.15), calls=%async_computation.1 | async-start | bytes 1310720 | tf_op jit(solution)/shard_map/all_to_all | solution.py:329
  32.4 4.0 %collective-permute-start = (bf16[16,160,128]{2,1,0:T(8,128)(2,1)S(1)}, bf16[16,160,128]{2,1,0:T(8,128)(2,1)S(1)}, u32[]{:S(2)}, u32[]{:S(2)}) collective-permute-start(bf16[16,160,128]{2,1,0:T(8,128)(2,1)S(1)} %all-to-all-done.1.mine_ref), channel_id=1, source_target_pairs={{0,1},{1,0},{2,3},{3,2},{4,5},{5,4},{6,7},{7,6},{8,9},{9,8},{10,11... | collective-permute-start | bytes 1966088 | tf_op jit(solution)/shard_map/ppermute | solution.py:331
  44.2 4.0 %collective-permute-start.1 = (bf16[16,160,128]{2,1,0:T(8,128)(2,1)S(1)}, bf16[16,160,128]{2,1,0:T(8,128)(2,1)S(1)}, u32[]{:S(2)}, u32[]{:S(2)}) collective-permute-start(bf16[16,160,128]{2,1,0:T(8,128)(2,1)S(1)} %get-tuple-element.14), channel_id=1, source_target_pairs={{0,1},{1,0},{2,3},{3,2},{4,5},{5,4},{6,7},{7,6},{8,9},{9,8},{10,11... | collective-permute-start | bytes 1966088 | tf_op jit(solution)/shard_map/ppermute | solution.py:333

commit v4 on v3

--- a/solution.py
+++ b/solution.py
@@ -89,9 +89,10 @@
             at = (n // 8) * (NC * WD) + n % 8 + c * WD + 8 * g
             t = own * NG + g
             perm[:, LANE * t : LANE * (t + 1)] = (row == at).astype(f32).astype(bf16)
+    x = [stream_ref[:, DZ * z : DZ * (z + 1)] for z in range(NZ)]
+    x = dot(jnp.concatenate(x, axis=0), perm[...]).astype(bf16)
     for z in range(NZ):
-        cols = slice(DZ * z, DZ * (z + 1))
-        stream_out[:, cols] = dot(stream_ref[:, cols], perm[...]).astype(bf16)
+        stream_out[:, DZ * z : DZ * (z + 1)] = x[TOK * z : TOK * (z + 1)]
 
 
 def hidden_kernel(hidden_ref, hidden_out):
@@ -113,7 +114,7 @@
 
 def main_kernel(
     teacher_ref, mine_ref, other_ref, hidden_hbm, stream_ref, keep_ref, send_ref,
-    hidden, a_out, gain, unit, rows, grad_out, grad_gain, sems,
+    hidden, a_out, gain, summed, rows, grad_out, grad_gain, sems,
 ):
     blocks = (mine_ref, other_ref)
     one = eye(LANE)
@@ -168,7 +169,7 @@
     for n in range(NCH):
         cols = slice(CH * n, CH * (n + 1))
         s = stream_ref[:, cols].astype(f32) + dot(low, a_out[:, cols])
-        unit[:, cols] = s
+        summed[:, cols] = s
         for g in range(NG):
             x = s[:, LANE * g : LANE * (g + 1)]
             squares = squares + x * x
@@ -178,8 +179,7 @@
     acc = jnp.zeros((TOK, LANE), f32)
     for n in range(NCH):
         cols = slice(CH * n, CH * (n + 1))
-        u = unit[:, cols] * inv
-        unit[:, cols] = u
+        u = summed[:, cols] * inv
         gn = gain[:1, cols]
         uq = jnp.sum(u[:QLEN], axis=0, keepdims=True) / QLEN
         up = jnp.sum(u[QLEN : QLEN + PLEN], axis=0, keepdims=True) / PLEN
@@ -198,27 +198,27 @@
         for g in range(NG):
             acc = acc + prod[:, LANE * g : LANE * (g + 1)]
     err = jnp.sum(margin, axis=1, keepdims=True) - teacher_ref[0]
-    mean = jnp.sum(acc, axis=1, keepdims=True) / D
+    mean = inv * (jnp.sum(acc, axis=1, keepdims=True) / D)
     scale = inv * err
 
     grad_gain[...] = jnp.zeros_like(grad_gain)
-    acc = jnp.zeros((R, TOK), f32)
+    acc = jnp.zeros((TOK, R), f32)
     for n in range(NCH):
         cols = slice(CH * n, CH * (n + 1))
-        um = unit[:, cols] * mean
+        um = summed[:, cols] * mean
         wq = rows[0:1, cols]
         wp = rows[1:2, cols]
         d = jnp.concatenate(
             [wq - um[:QLEN], wp - um[QLEN : QLEN + PLEN], -wp - um[QLEN + PLEN :]], axis=0
         )
         d = (d * scale).astype(bf16)
-        acc = acc + dot_t(a_out[:, cols], d)
+        acc = acc + dot_t(d, a_out[:, cols])
         grad_out[:, cols] = dot(low_t, d).astype(bf16)
         gg = 2.0 * err * rows[2:3, cols]
         for g in range(NG):
             row = GAIN - LANE + 16 + g
             grad_gain[row : row + 1, LANE * n : LANE * (n + 1)] = gg[:, LANE * g : LANE * (g + 1)]
-    d_low = acc.astype(bf16)
+    d_low = dot_t(eye(R), acc.astype(bf16)).astype(bf16)
 
     outs = (keep_ref, send_ref)
     for own in (1, 0):
@@ -244,7 +244,7 @@
 
 
 def final_kernel(in_ref, a_ref, o_ref, g_ref):
-    b = in_ref[...]
+    b = jnp.sum(in_ref[...].astype(f32), axis=0)
     a_ref[...] = b[:R, :WF]
     low = b[R:]
     n = lanes(8)
@@ -321,13 +321,14 @@
         scratch_shapes=[pltpu.VMEM((R, LANE), f32), pltpu.VMEM((LANE, LANE), f32)],
     )
     column = lax.all_to_all(mine, "zl", 0, 0, tiled=True)
-    column, stream = lax.optimization_barrier((column, place_stream(stream)))
     column = jnp.concatenate(
         [column[:, :R].reshape(1, TOP, LANE), column[:, R:].reshape(1, 8 * NZ, LANE)], axis=1
     )
     copies = jnp.broadcast_to(column, (NXY, NZ * BLK, LANE))
     mine = lax.all_to_all(copies, ("x", "y"), 0, 0, tiled=True)
-    mine, hidden = lax.optimization_barrier((mine, place_hidden(hidden)))
+    mine, hidden, stream = lax.optimization_barrier(
+        (mine, place_hidden(hidden), place_stream(stream))
+    )
     other = lax.ppermute(mine, "c", SWAP)
     keep, send = local(teacher, mine, other, hidden, stream)
     other = lax.ppermute(send, "c", SWAP)
@@ -340,7 +341,7 @@
     parts = jnp.broadcast_to(part, (NH, NZ, BLK, LANE)).reshape(NH * NZ, BLK, LANE)
     parts = lax.all_to_all(parts, ("zh", "zl"), 0, 0, tiled=True)
     shapes = (shape(R, WF, dtype=f32), shape(R, WD, dtype=f32), shape(1, WD, dtype=f32))
-    return call(final_kernel, shapes, jnp.sum(parts.astype(f32), axis=0))
+    return call(final_kernel, shapes, parts)
 
 
 def solution(mesh):

time: 94.9 us -> 94.4 us (level)
  blocking collectives: 43.7 us -> 57.4 us
  starting transfers between devices: 17 us -> 8.27 us
  waiting for transfers between devices: 10.5 us -> 7.29 us
  local copies, waits for them, and re-layouts: 2.28 us -> 0.97 us
    all_to_all x0 -> x1, blocking collectives: none -> 13.2 us  [body(): column = lax.all_to_all(mine, 'zl', 0, 0, tiled=True)]
    all_to_all x1 -> x0, starting transfers between devices: 8.72 us -> none  [body(): column = lax.all_to_all(mine, 'zl', 0, 0, tiled=True)]
    all_to_all x1, waiting for transfers between devices: 6.61 us -> 3.94 us  [body(): mine = lax.all_to_all(copies, ('x', 'y'), 0, 0, tiled=True)]
    unnamed x2, local copies, waits for them, and re-layouts: 1.32 us -> 0.01 us
  transfers between devices with their start and end apart: 4 -> 3, of which waited for: 4 -> 3; matrix products, arithmetic and copies ran while one was open for 0% -> 0% of each run, Pallas kernels for 8% -> 8%
where the time goes in v4:
time: 94.4 us; the launch traced here: 93.9 us
  blocking collectives  57.4 us (61%)
  Pallas kernels  18.3 us (19%)
  starting transfers between devices  8.27 us (9%)
  waiting for transfers between devices  7.29 us (8%)
  between operations  1.36 us (1%)
  local copies, waits for them, and re-layouts  0.97 us (1%)
    all_to_all x1, blocking collectives, body(): parts = lax.all_to_all(parts, ('zh', 'zl'), 0, 0, tiled=True)  27.9 us
    pallas_call x5, Pallas kernels, call(): pl.pallas_call(kernel, out_shape=shapes, in_specs=in_specs or [VMEM] * le...  18.3 us
    all_to_all x1, blocking collectives, body(): parts = lax.all_to_all(pairs, ('x', 'y'), 0, 0, tiled=True)  16.3 us
    all_to_all x1, blocking collectives, body(): column = lax.all_to_all(mine, 'zl', 0, 0, tiled=True)  13.2 us
    all_to_all x1, starting transfers between devices, body(): mine = lax.all_to_all(copies, ('x', 'y'), 0, 0, tiled=True)  4.32 us
    all_to_all x1, waiting for transfers between devices, body(): mine = lax.all_to_all(copies, ('x', 'y'), 0, 0, tiled=True)  3.94 us
    ppermute x1, starting transfers between devices, body(): other = lax.ppermute(send, 'c', SWAP)  2.05 us
    ppermute x1, waiting for transfers between devices, body(): other = lax.ppermute(send, 'c', SWAP)  1.94 us
  transfers between devices with their start and end apart: 3, of which 3 were waited for; matrix products, arithmetic and copies ran while one was open for 0% of the time, Pallas kernels for 8%

profile of v4, /device:TPU:32, one launch (start us, length us, event | category | flops | bytes accessed | tf_op | source)
XLA Modules:
  0.0 93.9 jit_solution(10574769619261081831)
XLA Ops:
  0.6 1.5 %shard_map.85 = bf16[4,40,128]{2,1,0:T(8,128)(2,1)} custom-call(bf16[32,108]{1,0:T(8,128)(2,1)} %a_ref.1, bf16[32,40]{1,0:T(8,128)(2,1)} %o_ref.1, f32[1,40]{1,0:T(1,128)} %g_ref.1), custom_call_target="tpu_custom_call" | custom-call | tf_op jit(solution)/shard_map/pallas_call | solution.py:266
  2.1 13.2 %all_to_all.20 = bf16[4,40,128]{2,1,0:T(8,128)(2,1)S(1)} all-to-all(bf16[4,40,128]{2,1,0:T(8,128)(2,1)} %shard_map.85), channel_id=1, replica_groups=mesh['zh'=4,'zl'=4,'x'=4,'y'=4,'c'=2] {'zl'}, dimensions={0} | all-to-all | bytes 81920 | tf_op jit(solution)/shard_map/all_to_all | solution.py:323
  15.3 0.9 broadcast_in_dim.15
  16.2 4.3 %all-to-all-start.1 = ((bf16[16,160,128]{2,1,0:T(8,128)(2,1)}), bf16[16,160,128]{2,1,0:T(8,128)(2,1)S(1)}, u32[]{:S(2)}, u32[]{:S(2)}) async-start(bf16[16,160,128]{2,1,0:T(8,128)(2,1)} %broadcast_in_dim.15), calls=%async_computation.1 | async-start | bytes 1310720 | tf_op jit(solution)/shard_map/all_to_all | solution.py:328
  20.5 0.0 copy-start
  20.5 5.4 %shard_map.86.hidden_hbm = bf16[2,4,128,2048]{3,2,1,0:T(8,128)(2,1)} custom-call(bf16[128,13824]{1,0:T(8,128)(2,1)} %hidden_ref.1), custom_call_target="tpu_custom_call" | custom-call | flops 14155776 | bytes 10616832 | tf_op jit(solution)/shard_map/pallas_call | solution.py:266
  25.9 0.0 copy-done
  25.9 2.1 %shard_map.87.stream_ref = bf16[128,5120]{1,0:T(8,128)(2,1)S(1)} custom-call(bf16[128,5120]{1,0:T(8,128)(2,1)S(1)} %copy-done), custom_call_target="tpu_custom_call" | custom-call | flops 1677721600 | bytes 2621440 | tf_op jit(solution)/shard_map/pallas_call | solution.py:266
  28.1 3.9 %all-to-all-done.1.mine_ref = bf16[16,160,128]{2,1,0:T(8,128)(2,1)S(1)} async-done(((bf16[16,160,128]{2,1,0:T(8,128)(2,1)}), bf16[16,160,128]{2,1,0:T(8,128)(2,1)S(1)}, u32[]{:S(2)}, u32[]{:S(2)}) %all-to-all-start.1) | async-done | bytes 655392 | tf_op jit(solution)/shard_map/all_to_all | solution.py:328
  32.0 1.9 %collective-permute-start = (bf16[16,160,128]{2,1,0:T(8,128)(2,1)S(1)}, bf16[16,160,128]{2,1,0:T(8,128)(2,1)S(1)}, u32[]{:S(2)}, u32[]{:S(2)}) collective-permute-start(bf16[16,160,128]{2,1,0:T(8,128)(2,1)S(1)} %all-to-all-done.1.mine_ref), channel_id=1, source_target_pairs={{0,1},{1,0},{2,3},{3,2},{4,5},{5,4},{6,7},{7,6},{8,9},{9,8},{10,11... | collective-permute-start | bytes 1966088 | tf_op jit(solution)/shard_map/ppermute | solution.py:332
  34.6 1.4 %collective-permute-done.other_ref = bf16[16,160,128]{2,1,0:T(8,128)(2,1)S(1)} collective-permute-done((bf16[16,160,128]{2,1,0:T(8,128)(2,1)S(1)}, bf16[16,160,128]{2,1,0:T(8,128)(2,1)S(1)}, u32[]{:S(2)}, u32[]{:S(2)}) %collective-permute-start) | collective-permute-done | bytes 655392 | tf_op jit(solution)/shard_map/ppermute | solution.py:332
  36.0 7.6 %shard_map.88 = (bf16[16,160,128]{2,1,0:T(8,128)(2,1)S(1)}, bf16[16,160,128]{2,1,0:T(8,128)(2,1)S(1)}) custom-call(f32[1]{0:T(128)S(6)} %copy.9.teacher_ref, bf16[16,160,128]{2,1,0:T(8,128)(2,1)S(1)} %all-to-all-done.1.mine_ref, bf16[16,160,128]{2,1,0:T(8,128)(2,1)S(1)} %collective-permute-done.other_ref, bf16[2,4,128,2048]{3,2,1,0:T(8,128)(2,1)} %shard_map.86.hidden_hbm, ...), custom_call_target="tpu_custom_call" | custom-call | tf_op jit(solution)/shard_map/pallas_call | solution.py:266
  43.6 2.0 %collective-permute-start.1 = (bf16[16,160,128]{2,1,0:T(8,128)(2,1)S(1)}, bf16[16,160,128]{2,1,0:T(8,128)(2,1)S(1)}, u32[]{:S(2)}, u32[]{:S(2)}) collective-permute-start(bf16[16,160,128]{2,1,0:T(8,128)(2,1)S(1)} %get-tuple-element.12), channel_id=1, source_target_pairs={{0,1},{1,0},{2,3},{3,2},{4,5},{5,4},{6,7},{7,6},{8,9},{9,8},{10,11... | collective-permute-start | bytes 1966088 | tf_op jit(solution)/shard_map/ppermute | solution.py:334
  45.7 1.9 %collective-permute-done.1 = bf16[16,160,128]{2,1,0:T(8,128)(2,1)S(1)} collective-permute-done((bf16[16,160,128]{2,1,0:T(8,128)(2,1)S(1)}, bf16[16,160,128]{2,1,0:T(8,128)(2,1)S(1)}, u32[]{:S(2)}, u32[]{:S(2)}) %collective-permute-start.1) | collective-permute-done | bytes 655392 | tf_op jit(solution)/shard_map/ppermute | solution.py:334
  47.6 0.2 add_convert_fusion
  47.8 16.3 %all_to_all.21 = bf16[16,160,128]{2,1,0:T(8,128)(2,1)S(1)} all-to-all(bf16[16,160,128]{2,1,0:T(8,128)(2,1)S(1)} %add_convert_fusion), channel_id=1, replica_groups=mesh['zh'=4,'zl'=4,'x'=4,'y'=4,'c'=2] {'x','y'}, dimensions={0} | all-to-all | bytes 1310720 | tf_op jit(solution)/shard_map/all_to_all | solution.py:336
  64.1 0.1 reduce_sum.12
  64.3 27.9 %all_to_all.22.in_ref = bf16[16,40,128]{2,1,0:T(8,128)(2,1)} all-to-all(bf16[16,40,128]{2,1,0:T(8,128)(2,1)S(1)} %bitcast.11), channel_id=1, replica_groups=mesh['zh'=4,'zl'=4,'x'=4,'y'=4,'c'=2] {'zh','zl'}, dimensions={0} | all-to-all | bytes 327680 | tf_op jit(solution)/shard_map/all_to_all | solution.py:342
  92.2 1.7 %shard_map.89 = (f32[32,108]{1,0:T(8,128)}, f32[32,40]{1,0:T(8,128)}, f32[1,40]{1,0:T(1,128)}) custom-call(bf16[16,40,128]{2,1,0:T(8,128)(2,1)} %all_to_all.22.in_ref), custom_call_target="tpu_custom_call" | custom-call | tf_op jit(solution)/shard_map/pallas_call | solution.py:266
  (7 shorter events, 0.1 us)
Async XLA Ops:
  16.2 15.8 %all-to-all-start.1 = ((bf16[16,160,128]{2,1,0:T(8,128)(2,1)}), bf16[16,160,128]{2,1,0:T(8,128)(2,1)S(1)}, u32[]{:S(2)}, u32[]{:S(2)}) async-start(bf16[16,160,128]{2,1,0:T(8,128)(2,1)} %broadcast_in_dim.15), calls=%async_computation.1 | async-start | bytes 1310720 | tf_op jit(solution)/shard_map/all_to_all | solution.py:328
  20.5 5.4 %copy-start = (bf16[128,5120]{1,0:T(8,128)(2,1)S(1)}, bf16[128,5120]{1,0:T(8,128)(2,1)}, u32[]{:S(2)}) copy-start(bf16[128,5120]{1,0:T(8,128)(2,1)} %stream_ref.1) | copy-start | bytes 3932164
  32.0 4.0 %collective-permute-start = (bf16[16,160,128]{2,1,0:T(8,128)(2,1)S(1)}, bf16[16,160,128]{2,1,0:T(8,128)(2,1)S(1)}, u32[]{:S(2)}, u32[]{:S(2)}) collective-permute-start(bf16[16,160,128]{2,1,0:T(8,128)(2,1)S(1)} %all-to-all-done.1.mine_ref), channel_id=1, source_target_pairs={{0,1},{1,0},{2,3},{3,2},{4,5},{5,4},{6,7},{7,6},{8,9},{9,8},{10,11... | collective-permute-start | bytes 1966088 | tf_op jit(solution)/shard_map/ppermute | solution.py:332
  43.6 4.0 %collective-permute-start.1 = (bf16[16,160,128]{2,1,0:T(8,128)(2,1)S(1)}, bf16[16,160,128]{2,1,0:T(8,128)(2,1)S(1)}, u32[]{:S(2)}, u32[]{:S(2)}) collective-permute-start(bf16[16,160,128]{2,1,0:T(8,128)(2,1)S(1)} %get-tuple-element.12), channel_id=1, source_target_pairs={{0,1},{1,0},{2,3},{3,2},{4,5},{5,4},{6,7},{7,6},{8,9},{9,8},{10,11... | collective-permute-start | bytes 1966088 | tf_op jit(solution)/shard_map/ppermute | solution.py:334

commit v5 on v4

--- a/solution.py
+++ b/solution.py
@@ -114,15 +114,15 @@
 
 def main_kernel(
     teacher_ref, mine_ref, other_ref, hidden_hbm, stream_ref, keep_ref, send_ref,
-    hidden, a_out, gain, summed, rows, grad_out, grad_gain, sems,
+    hidden, a_out, gain, summed, rows, grad_out, grad_gain, d_all, sems,
 ):
     blocks = (mine_ref, other_ref)
     one = eye(LANE)
     k8 = 8
-    n = NXY * LANE
-    spread = lax.broadcasted_iota(jnp.int32, (LANE, n), 0)
-    spread = spread // 8 * LANE + spread % 8 + LAST
-    spread = (spread == lax.broadcasted_iota(jnp.int32, (LANE, n), 1)).astype(f32).astype(bf16)
+    at = lax.broadcasted_iota(jnp.int32, (LANE, LANE), 0)
+    at = (at >> 3) * LANE + (at & 7) + LAST - lanes(LANE)
+    spread = [(at == LANE * i).astype(f32).astype(bf16) for i in range(NXY)]
+    spread = jnp.concatenate(spread, axis=1)
     copies = {}
     for own in range(NC):
         for z in range(NZ):
@@ -202,7 +202,6 @@
     scale = inv * err
 
     grad_gain[...] = jnp.zeros_like(grad_gain)
-    acc = jnp.zeros((TOK, R), f32)
     for n in range(NCH):
         cols = slice(CH * n, CH * (n + 1))
         um = summed[:, cols] * mean
@@ -212,13 +211,13 @@
             [wq - um[:QLEN], wp - um[QLEN : QLEN + PLEN], -wp - um[QLEN + PLEN :]], axis=0
         )
         d = (d * scale).astype(bf16)
-        acc = acc + dot_t(d, a_out[:, cols])
+        d_all[:, cols] = d
         grad_out[:, cols] = dot(low_t, d).astype(bf16)
         gg = 2.0 * err * rows[2:3, cols]
         for g in range(NG):
             row = GAIN - LANE + 16 + g
             grad_gain[row : row + 1, LANE * n : LANE * (n + 1)] = gg[:, LANE * g : LANE * (g + 1)]
-    d_low = dot_t(eye(R), acc.astype(bf16)).astype(bf16)
+    d_low = dot_t(eye(R), dot_t(d_all[...], a_out[...]).astype(bf16)).astype(bf16)
 
     outs = (keep_ref, send_ref)
     for own in (1, 0):
@@ -309,6 +308,7 @@
             pltpu.VMEM((8, D), f32),
             pltpu.VMEM((R, D), bf16),
             pltpu.VMEM((16, NCH * LANE), f32),
+            pltpu.VMEM((TOK, D), bf16),
             pltpu.SemaphoreType.DMA((NC * NZ,)),
         ],
         limit=49 * 2**20,

time: 94.4 us -> 94.6 us (level)
  no operation moved by 1% of the time
where the time goes in v5:
time: 94.6 us; the launch traced here: 94 us
  blocking collectives  57.4 us (61%)
  Pallas kernels  18.5 us (20%)
  starting transfers between devices  8.27 us (9%)
  waiting for transfers between devices  7.29 us (8%)
  between operations  1.36 us (1%)
  local copies, waits for them, and re-layouts  0.97 us (1%)
    all_to_all x1, blocking collectives, body(): parts = lax.all_to_all(parts, ('zh', 'zl'), 0, 0, tiled=True)  27.9 us
    pallas_call x5, Pallas kernels, call(): pl.pallas_call(kernel, out_shape=shapes, in_specs=in_specs or [VMEM] * le...  18.5 us
    all_to_all x1, blocking collectives, body(): parts = lax.all_to_all(pairs, ('x', 'y'), 0, 0, tiled=True)  16.3 us
    all_to_all x1, blocking collectives, body(): column = lax.all_to_all(mine, 'zl', 0, 0, tiled=True)  13.2 us
    all_to_all x1, starting transfers between devices, body(): mine = lax.all_to_all(copies, ('x', 'y'), 0, 0, tiled=True)  4.32 us
    all_to_all x1, waiting for transfers between devices, body(): mine = lax.all_to_all(copies, ('x', 'y'), 0, 0, tiled=True)  3.94 us
    ppermute x1, starting transfers between devices, body(): other = lax.ppermute(send, 'c', SWAP)  2.05 us
    ppermute x1, waiting for transfers between devices, body(): other = lax.ppermute(send, 'c', SWAP)  1.94 us
  transfers between devices with their start and end apart: 3, of which 3 were waited for; matrix products, arithmetic and copies ran while one was open for 0% of the time, Pallas kernels for 8%

profile of v5, /device:TPU:32, one launch (start us, length us, event | category | flops | bytes accessed | tf_op | source)
XLA Modules:
  0.0 94.0 jit_solution(13890929309028250466)
XLA Ops:
  0.6 1.5 %shard_map.85 = bf16[4,40,128]{2,1,0:T(8,128)(2,1)} custom-call(bf16[32,108]{1,0:T(8,128)(2,1)} %a_ref.1, bf16[32,40]{1,0:T(8,128)(2,1)} %o_ref.1, f32[1,40]{1,0:T(1,128)} %g_ref.1), custom_call_target="tpu_custom_call" | custom-call | tf_op jit(solution)/shard_map/pallas_call | solution.py:265
  2.1 13.2 %all_to_all.20 = bf16[4,40,128]{2,1,0:T(8,128)(2,1)S(1)} all-to-all(bf16[4,40,128]{2,1,0:T(8,128)(2,1)} %shard_map.85), channel_id=1, replica_groups=mesh['zh'=4,'zl'=4,'x'=4,'y'=4,'c'=2] {'zl'}, dimensions={0} | all-to-all | bytes 81920 | tf_op jit(solution)/shard_map/all_to_all | solution.py:323
  15.3 0.9 broadcast_in_dim.15
  16.2 4.3 %all-to-all-start.1 = ((bf16[16,160,128]{2,1,0:T(8,128)(2,1)}), bf16[16,160,128]{2,1,0:T(8,128)(2,1)S(1)}, u32[]{:S(2)}, u32[]{:S(2)}) async-start(bf16[16,160,128]{2,1,0:T(8,128)(2,1)} %broadcast_in_dim.15), calls=%async_computation.1 | async-start | bytes 1310720 | tf_op jit(solution)/shard_map/all_to_all | solution.py:328
  20.5 0.0 copy-start
  20.5 5.4 %shard_map.86.hidden_hbm = bf16[2,4,128,2048]{3,2,1,0:T(8,128)(2,1)} custom-call(bf16[128,13824]{1,0:T(8,128)(2,1)} %hidden_ref.1), custom_call_target="tpu_custom_call" | custom-call | flops 14155776 | bytes 10616832 | tf_op jit(solution)/shard_map/pallas_call | solution.py:265
  25.9 0.0 copy-done
  25.9 2.1 %shard_map.87.stream_ref = bf16[128,5120]{1,0:T(8,128)(2,1)S(1)} custom-call(bf16[128,5120]{1,0:T(8,128)(2,1)S(1)} %copy-done), custom_call_target="tpu_custom_call" | custom-call | flops 1677721600 | bytes 2621440 | tf_op jit(solution)/shard_map/pallas_call | solution.py:265
  28.1 3.9 %all-to-all-done.1.mine_ref = bf16[16,160,128]{2,1,0:T(8,128)(2,1)S(1)} async-done(((bf16[16,160,128]{2,1,0:T(8,128)(2,1)}), bf16[16,160,128]{2,1,0:T(8,128)(2,1)S(1)}, u32[]{:S(2)}, u32[]{:S(2)}) %all-to-all-start.1) | async-done | bytes 655392 | tf_op jit(solution)/shard_map/all_to_all | solution.py:328
  32.0 1.9 %collective-permute-start = (bf16[16,160,128]{2,1,0:T(8,128)(2,1)S(1)}, bf16[16,160,128]{2,1,0:T(8,128)(2,1)S(1)}, u32[]{:S(2)}, u32[]{:S(2)}) collective-permute-start(bf16[16,160,128]{2,1,0:T(8,128)(2,1)S(1)} %all-to-all-done.1.mine_ref), channel_id=1, source_target_pairs={{0,1},{1,0},{2,3},{3,2},{4,5},{5,4},{6,7},{7,6},{8,9},{9,8},{10,11... | collective-permute-start | bytes 1966088 | tf_op jit(solution)/shard_map/ppermute | solution.py:332
  34.6 1.4 %collective-permute-done.other_ref = bf16[16,160,128]{2,1,0:T(8,128)(2,1)S(1)} collective-permute-done((bf16[16,160,128]{2,1,0:T(8,128)(2,1)S(1)}, bf16[16,160,128]{2,1,0:T(8,128)(2,1)S(1)}, u32[]{:S(2)}, u32[]{:S(2)}) %collective-permute-start) | collective-permute-done | bytes 655392 | tf_op jit(solution)/shard_map/ppermute | solution.py:332
  36.0 7.8 %shard_map.88 = (bf16[16,160,128]{2,1,0:T(8,128)(2,1)S(1)}, bf16[16,160,128]{2,1,0:T(8,128)(2,1)S(1)}) custom-call(f32[1]{0:T(128)S(6)} %copy.9.teacher_ref, bf16[16,160,128]{2,1,0:T(8,128)(2,1)S(1)} %all-to-all-done.1.mine_ref, bf16[16,160,128]{2,1,0:T(8,128)(2,1)S(1)} %collective-permute-done.other_ref, bf16[2,4,128,2048]{3,2,1,0:T(8,128)(2,1)} %shard_map.86.hidden_hbm, ...), custom_call_target="tpu_custom_call" | custom-call | tf_op jit(solution)/shard_map/pallas_call | solution.py:265
  43.8 2.0 %collective-permute-start.1 = (bf16[16,160,128]{2,1,0:T(8,128)(2,1)S(1)}, bf16[16,160,128]{2,1,0:T(8,128)(2,1)S(1)}, u32[]{:S(2)}, u32[]{:S(2)}) collective-permute-start(bf16[16,160,128]{2,1,0:T(8,128)(2,1)S(1)} %get-tuple-element.12), channel_id=1, source_target_pairs={{0,1},{1,0},{2,3},{3,2},{4,5},{5,4},{6,7},{7,6},{8,9},{9,8},{10,11... | collective-permute-start | bytes 1966088 | tf_op jit(solution)/shard_map/ppermute | solution.py:334
  45.8 1.9 %collective-permute-done.1 = bf16[16,160,128]{2,1,0:T(8,128)(2,1)S(1)} collective-permute-done((bf16[16,160,128]{2,1,0:T(8,128)(2,1)S(1)}, bf16[16,160,128]{2,1,0:T(8,128)(2,1)S(1)}, u32[]{:S(2)}, u32[]{:S(2)}) %collective-permute-start.1) | collective-permute-done | bytes 655392 | tf_op jit(solution)/shard_map/ppermute | solution.py:334
  47.8 0.2 add_convert_fusion
  47.9 16.3 %all_to_all.21 = bf16[16,160,128]{2,1,0:T(8,128)(2,1)S(1)} all-to-all(bf16[16,160,128]{2,1,0:T(8,128)(2,1)S(1)} %add_convert_fusion), channel_id=1, replica_groups=mesh['zh'=4,'zl'=4,'x'=4,'y'=4,'c'=2] {'x','y'}, dimensions={0} | all-to-all | bytes 1310720 | tf_op jit(solution)/shard_map/all_to_all | solution.py:336
  64.2 0.1 reduce_sum.12
  64.4 27.9 %all_to_all.22.in_ref = bf16[16,40,128]{2,1,0:T(8,128)(2,1)} all-to-all(bf16[16,40,128]{2,1,0:T(8,128)(2,1)S(1)} %bitcast.11), channel_id=1, replica_groups=mesh['zh'=4,'zl'=4,'x'=4,'y'=4,'c'=2] {'zh','zl'}, dimensions={0} | all-to-all | bytes 327680 | tf_op jit(solution)/shard_map/all_to_all | solution.py:342
  92.3 1.7 %shard_map.89 = (f32[32,108]{1,0:T(8,128)}, f32[32,40]{1,0:T(8,128)}, f32[1,40]{1,0:T(1,128)}) custom-call(bf16[16,40,128]{2,1,0:T(8,128)(2,1)} %all_to_all.22.in_ref), custom_call_target="tpu_custom_call" | custom-call | tf_op jit(solution)/shard_map/pallas_call | solution.py:265
  (7 shorter events, 0.1 us)
Async XLA Ops:
  16.2 15.8 %all-to-all-start.1 = ((bf16[16,160,128]{2,1,0:T(8,128)(2,1)}), bf16[16,160,128]{2,1,0:T(8,128)(2,1)S(1)}, u32[]{:S(2)}, u32[]{:S(2)}) async-start(bf16[16,160,128]{2,1,0:T(8,128)(2,1)} %broadcast_in_dim.15), calls=%async_computation.1 | async-start | bytes 1310720 | tf_op jit(solution)/shard_map/all_to_all | solution.py:328
  20.5 5.4 %copy-start = (bf16[128,5120]{1,0:T(8,128)(2,1)S(1)}, bf16[128,5120]{1,0:T(8,128)(2,1)}, u32[]{:S(2)}) copy-start(bf16[128,5120]{1,0:T(8,128)(2,1)} %stream_ref.1) | copy-start | bytes 3932164
  32.0 4.0 %collective-permute-start = (bf16[16,160,128]{2,1,0:T(8,128)(2,1)S(1)}, bf16[16,160,128]{2,1,0:T(8,128)(2,1)S(1)}, u32[]{:S(2)}, u32[]{:S(2)}) collective-permute-start(bf16[16,160,128]{2,1,0:T(8,128)(2,1)S(1)} %all-to-all-done.1.mine_ref), channel_id=1, source_target_pairs={{0,1},{1,0},{2,3},{3,2},{4,5},{5,4},{6,7},{7,6},{8,9},{9,8},{10,11... | collective-permute-start | bytes 1966088 | tf_op jit(solution)/shard_map/ppermute | solution.py:332
  43.8 4.0 %collective-permute-start.1 = (bf16[16,160,128]{2,1,0:T(8,128)(2,1)S(1)}, bf16[16,160,128]{2,1,0:T(8,128)(2,1)S(1)}, u32[]{:S(2)}, u32[]{:S(2)}) collective-permute-start(bf16[16,160,128]{2,1,0:T(8,128)(2,1)S(1)} %get-tuple-element.12), channel_id=1, source_target_pairs={{0,1},{1,0},{2,3},{3,2},{4,5},{5,4},{6,7},{7,6},{8,9},{9,8},{10,11... | collective-permute-start | bytes 1966088 | tf_op jit(solution)/shard_map/ppermute | solution.py:334
